TPU v7x, 256 devices: a whole 4x4x8 slice. The times are simulated.
256 devices in a mesh: exp: 32 (over z, y), head: 8 (over x, core).
Axes of the slice: x: 4, y: 4, z: 8, core: 2. Of those that a mesh axis runs over, the one named last changes fastest.
Arguments:
- tokens: bfloat16 [4096, 4096], P('exp', 'head'), may hold values from -6 to 6
- cotangent: bfloat16 [4096, 4096], P('exp', 'head'), may hold values from -3 to 3
- gates: bfloat16 [4096, 2], P('exp'), may hold values from 0.099609375 to 1
- expert_ids: int32 [4096, 2], P('exp'), may hold values from 0 to 31, all different within a row; in each aligned block of 128 rows (0 to 127, 128 to 255, ...) at most 16 rows name the same one
- w_up: bfloat16 [32, 4096, 2048], P('exp', None, 'head'), may hold values from -0.09375 to 0.09375
- w_down: bfloat16 [32, 2048, 4096], P('exp', 'head'), may hold values from -0.125 to 0.125
Outputs:
- grad_tokens: bfloat16 [4096, 4096], P('exp', 'head')
- grad_gates: bfloat16 [4096, 2], P('exp')
- grad_up: bfloat16 [32, 4096, 2048], P('exp', None, 'head')
- grad_down: bfloat16 [32, 2048, 4096], P('exp', 'head')
Inputs may be any that keep to these rules, and one draw needn't show every extreme that they name: `expert_ids`: the two experts of a token differ; among the tokens of one index of exp, no expert is named more than 16 times, and in every draw some expert is named exactly 16 times by the tokens of some index.
All inputs are finite; a program needn't handle non-finite values.
Results may differ from a plain program's by a relative error of at most 0.0058.
Values may be sent and summed in bfloat16 or wider, within the bound.
A program may use at most 128 MiB of HBM per device.

v0:
```python
import math

import jax
import jax.numpy as jnp
from jax import lax
from jax.sharding import PartitionSpec as P


def gelu_parts(pre):
    phi = 0.5 * (1.0 + lax.erf(pre / math.sqrt(2.0)))
    act = pre * phi
    slope = phi + pre * jnp.exp(-0.5 * pre * pre) / math.sqrt(2.0 * math.pi)
    return (act, slope)


def contract_rows(left, right):
    return lax.dot_general(
        left, right, (((0,), (0,)), ((), ())), preferred_element_type=jnp.float32
    )


def shards(tokens, cotangent, gates, expert_ids, w_up, w_down):
    tok_rows = tokens.shape[0]
    experts = lax.axis_size("exp")
    capacity = 4 * tok_rows // experts
    flat = expert_ids.reshape(2 * tok_rows)
    onehot = (flat[:, None] == jnp.arange(experts, dtype=jnp.int32)[None, :]).astype(jnp.int32)
    before = jnp.cumsum(onehot, axis=0) - onehot
    slot = jnp.sum(before * onehot, axis=1)
    dest = flat * capacity + slot
    placed = (dest[None, :] == jnp.arange(experts * capacity, dtype=jnp.int32)[:, None]).astype(
        jnp.bfloat16
    )
    picker = jnp.sum(placed.reshape(experts * capacity, tok_rows, 2), axis=2)
    gate_send = jnp.dot(placed, gates.reshape(2 * tok_rows, 1), preferred_element_type=jnp.float32)
    gate_send = gate_send.reshape(experts * capacity).astype(jnp.bfloat16)
    x_whole, dy_whole = (
        lax.all_gather(tokens, "head", axis=1, tiled=True),
        lax.all_gather(cotangent, "head", axis=1, tiled=True),
    )
    x_send = jnp.dot(picker, x_whole, preferred_element_type=jnp.float32).astype(jnp.bfloat16)
    dy_send = jnp.dot(picker, dy_whole, preferred_element_type=jnp.float32).astype(jnp.bfloat16)
    x_rows, dy_rows, g_rows = (
        lax.all_to_all(x_send, "exp", split_axis=0, concat_axis=0, tiled=True),
        lax.all_to_all(dy_send, "exp", split_axis=0, concat_axis=0, tiled=True),
        lax.all_to_all(gate_send, "exp", split_axis=0, concat_axis=0, tiled=True),
    )
    weight_up = w_up[0]
    weight_down = w_down[0]
    g_column = g_rows.astype(jnp.float32)[:, None]
    pre = jnp.dot(x_rows, weight_up, preferred_element_type=jnp.float32)
    back = lax.dot_general(
        dy_rows, weight_down, (((1,), (1,)), ((), ())), preferred_element_type=jnp.float32
    )
    act, slope = gelu_parts(pre)
    score_part = jnp.sum(back * act, axis=1)
    scaled = (g_column * act).astype(jnp.bfloat16)
    delta = (g_column * back * slope).astype(jnp.bfloat16)
    grad_down = contract_rows(scaled, dy_rows).astype(jnp.bfloat16)
    grad_up = contract_rows(x_rows, delta).astype(jnp.bfloat16)
    row_terms = lax.dot_general(
        delta, weight_up, (((1,), (1,)), ((), ())), preferred_element_type=jnp.float32
    )
    row_grad = lax.psum_scatter(row_terms, "head", scatter_dimension=1, tiled=True).astype(
        jnp.bfloat16
    )
    score = lax.psum(score_part, "head").astype(jnp.bfloat16)
    back_rows, back_score = (
        lax.all_to_all(row_grad, "exp", split_axis=0, concat_axis=0, tiled=True),
        lax.all_to_all(score, "exp", split_axis=0, concat_axis=0, tiled=True),
    )
    grad_tokens = contract_rows(picker, back_rows).astype(jnp.bfloat16)
    grad_gates = contract_rows(placed, back_score.reshape(experts * capacity, 1))
    grad_gates = grad_gates.reshape(tok_rows, 2).astype(jnp.bfloat16)
    return (grad_tokens, grad_gates, grad_up[None], grad_down[None])


def solution(mesh):
    return jax.shard_map(
        shards,
        mesh=mesh,
        in_specs=(
            P("exp", "head"),
            P("exp", "head"),
            P("exp", None),
            P("exp", None),
            P("exp", None, "head"),
            P("exp", "head", None),
        ),
        out_specs=(
            P("exp", "head"),
            P("exp", None),
            P("exp", None, "head"),
            P("exp", "head", None),
        ),
        check_vma=False,
    )
```

profile of v0, /device:TPU:2, one launch (start us, length us, event | category | flops | bytes accessed | tf_op | source)
XLA Modules:
  0.0 347.0 jit_solution(2725374376470468580)
XLA Ops:
  7.2 0.7 all-gather.5.cloned.1.call-update
  7.9 0.8 copy.46
  9.0 0.8 copy.50
  9.9 0.6 reduce-window.6
  10.9 0.5 fusion.18
  11.5 0.7 copy.51
  12.2 11.5 %all-to-all-start = ((bf16[32,16,1]{1,2,0:T(2,128)(2,1)}), bf16[32,16,1]{1,2,0:T(2,128)(2,1)S(1)}, u32[]{:S(2)}, u32[]{:S(2)}) async-start(bf16[32,16,1]{1,2,0:T(2,128)(2,1)} %copy.51), calls=%async_computation | async-start | bytes 32768 | tf_op jit(solution)/shard_map/all_to_all | solution.py:46
  23.9 0.7 multiply_add_fusion.2
  24.6 12.6 %all-gather.5.cloned.1.call-done = bf16[128,4096]{1,0:T(8,128)(2,1)} async-done(((bf16[128,512]{1,0:T(8,128)(2,1)}), bf16[128,4096]{1,0:T(8,128)(2,1)}) %all-gather.5.cloned.1.call-update) | async-done | bytes 1048592 | tf_op jit(solution)/shard_map/all_gather | solution.py:38
  37.2 4.4 %convolution_convert_fusion = bf16[512,4096]{1,0:T(8,128)(2,1)} fusion(bf16[512,128]{1,0:T(8,128)(2,1)S(1)} %fusion.20, bf16[128,4096]{1,0:T(8,128)(2,1)} %all-gather.5.cloned.1.call-done), kind=kOutput, calls=%fused_computation | convolution fusion | flops 538968064 | bytes 5373952 | tf_op jit(solution)/shard_map/dot_general | solution.py:41
  41.6 9.8 %all-to-all-start.2 = ((bf16[32,16,4096]{2,1,0:T(8,128)(2,1)}), bf16[32,16,4096]{2,1,0:T(8,128)(2,1)}, u32[]{:S(2)}, u32[]{:S(2)}) async-start(bf16[32,16,4096]{2,1,0:T(8,128)(2,1)} %bitcast.63), calls=%async_computation.2 | async-start | bytes 8388608 | tf_op jit(solution)/shard_map/all_to_all | solution.py:44
  51.5 0.7 all-gather.3.cloned.1.call-update
  52.2 27.6 %all-gather.3.cloned.1.call-done = bf16[128,4096]{1,0:T(8,128)(2,1)} async-done(((bf16[128,512]{1,0:T(8,128)(2,1)}), bf16[128,4096]{1,0:T(8,128)(2,1)}) %all-gather.3.cloned.1.call-update) | async-done | bytes 1048592 | tf_op jit(solution)/shard_map/all_gather | solution.py:39
  79.8 4.4 %convolution_convert_fusion.1 = bf16[512,4096]{1,0:T(8,128)(2,1)} fusion(bf16[512,128]{1,0:T(8,128)(2,1)S(1)} %fusion.20, bf16[128,4096]{1,0:T(8,128)(2,1)} %all-gather.3.cloned.1.call-done), kind=kOutput, calls=%fused_computation.1 | convolution fusion | flops 538968064 | bytes 5373952 | tf_op jit(solution)/shard_map/dot_general | solution.py:42
  84.2 63.6 %all-to-all-done.2 = bf16[32,16,4096]{2,1,0:T(8,128)(2,1)} async-done(((bf16[32,16,4096]{2,1,0:T(8,128)(2,1)}), bf16[32,16,4096]{2,1,0:T(8,128)(2,1)}, u32[]{:S(2)}, u32[]{:S(2)}) %all-to-all-start.2) | async-done | bytes 4194336 | tf_op jit(solution)/shard_map/all_to_all | solution.py:44
  147.8 5.9 %all-to-all-start.1 = ((bf16[32,16,4096]{2,1,0:T(8,128)(2,1)}), bf16[32,16,4096]{2,1,0:T(8,128)(2,1)}, u32[]{:S(2)}, u32[]{:S(2)}) async-start(bf16[32,16,4096]{2,1,0:T(8,128)(2,1)} %bitcast.64), calls=%async_computation.1 | async-start | bytes 8388608 | tf_op jit(solution)/shard_map/all_to_all | solution.py:45
  153.9 3.5 %fusion.4 = f32[512,256]{0,1:T(8,128)S(1)} fusion(bf16[512,4096]{1,0:T(8,128)(2,1)} %bitcast.7, bf16[1,4096,256]{2,1,0:T(8,128)(2,1)S(1)} %copy-done), kind=kOutput, calls=%fused_computation.8 | convolution fusion | flops 1073741824 | bytes 6815744 | tf_op jit(solution)/shard_map/dot_general | solution.py:51
  157.4 90.6 %all-to-all-done.1 = bf16[32,16,4096]{2,1,0:T(8,128)(2,1)} async-done(((bf16[32,16,4096]{2,1,0:T(8,128)(2,1)}), bf16[32,16,4096]{2,1,0:T(8,128)(2,1)}, u32[]{:S(2)}, u32[]{:S(2)}) %all-to-all-start.1) | async-done | bytes 4194336 | tf_op jit(solution)/shard_map/all_to_all | solution.py:45
  248.0 4.2 %multiply_reduce_fusion = (f32[512]{0:T(512)S(1)}, f32[512,256]{0,1:T(8,128)S(1)}) fusion(f32[512,256]{0,1:T(8,128)S(1)} %fusion.4, bf16[512,4096]{1,0:T(8,128)(2,1)} %bitcast.4, bf16[1,256,4096]{2,1,0:T(8,128)(2,1)} %param.11), kind=kOutput, calls=%fused_computation.21 | convolution fusion | flops 1074527744 | bytes 7342080 | tf_op jit(solution)/shard_map/dot_general | solution.py:52
  252.2 0.8 copy-done.1
  253.0 4.7 %fusion.2 = f32[512,4096]{1,0:T(8,128)} fusion(bf16[1,4096,256]{2,1,0:T(8,128)(2,1)S(1)} %copy-done, f32[512,256]{0,1:T(8,128)S(1)} %fusion.4, f32[512,256]{0,1:T(8,128)S(1)} %get-tuple-element.5, f32[512]{0:T(512)S(1)} %reshape.119), kind=kOutput, calls=%fused_computation.6 | convolution fusion | flops 1075183616 | bytes 11536384 | tf_op jit(solution)/shard_map/dot_general | solution.py:61
  257.7 11.2 %psum.7 = bf16[512]{0:T(512)(128)(2,1)S(1)} all-reduce(f32[512]{0:T(512)S(1)} %get-tuple-element.4), channel_id=1, replica_groups=mesh['exp'=32,'head'=8] {'head'}, use_global_device_ids=true, to_apply=%region_6.7 | all-reduce | flops 512 | bytes 3072 | tf_op jit(solution)/shard_map/psum | solution.py:67
  268.9 0.7 all_to_all.46
  269.6 7.7 %all-to-all-start.4 = ((bf16[32,16,1]{1,2,0:T(2,128)(2,1)}), bf16[32,16,1]{1,2,0:T(2,128)(2,1)S(1)}, u32[]{:S(2)}, u32[]{:S(2)}) async-start(bf16[32,16,1]{1,2,0:T(2,128)(2,1)} %all_to_all.46), calls=%async_computation.5 | async-start | bytes 32768 | tf_op jit(solution)/shard_map/all_to_all | solution.py:70
  277.2 32.0 %reduce-scatter.2.cloned.1.call-done = f32[512,512]{1,0:T(8,128)} async-done(((f32[512,4096]{1,0:T(8,128)}), f32[512,512]{1,0:T(8,128)}) %reduce-scatter.2.cloned.1.call-update) | async-done | bytes 1048592 | tf_op jit(solution)/shard_map/reduce_scatter | solution.py:64
  309.2 2.1 convert_element_type.70
  311.3 10.2 %all-to-all-start.3 = ((bf16[32,16,512]{2,1,0:T(8,128)(2,1)}), bf16[32,16,512]{2,1,0:T(8,128)(2,1)S(1)}, u32[]{:S(2)}, u32[]{:S(2)}) async-start(bf16[32,16,512]{2,1,0:T(8,128)(2,1)} %bitcast.9), calls=%async_computation.4 | async-start | bytes 1048576 | tf_op jit(solution)/shard_map/all_to_all | solution.py:69
  321.6 4.8 %fusion.1 = bf16[1,256,4096]{2,1,0:T(8,128)(2,1)} fusion(bf16[512,4096]{1,0:T(8,128)(2,1)} %bitcast.4, f32[512]{0:T(512)S(1)} %reshape.119, f32[512,256]{0,1:T(8,128)S(1)} %fusion.4), kind=kOutput, calls=%fused_computation.5 | convolution fusion | flops 1075576832 | bytes 6817792 | tf_op jit(solution)/shard_map/dot_general | solution.py:17
  326.4 5.0 %fusion = bf16[1,4096,256]{2,1,0:T(8,128)(2,1)} fusion(bf16[512,4096]{1,0:T(8,128)(2,1)} %bitcast.7, f32[512,256]{0,1:T(8,128)S(1)} %fusion.4, f32[512,256]{0,1:T(8,128)S(1)} %copy-done.2, f32[512]{0:T(512)S(1)} %reshape.119), kind=kOutput, calls=%fused_computation.4 | convolution fusion | flops 1076232192 | bytes 7342080 | tf_op jit(solution)/shard_map/dot_general | solution.py:17
  331.8 0.5 convert_element_type.73
  332.3 7.2 %all-to-all-done.3 = bf16[32,16,512]{2,1,0:T(8,128)(2,1)S(1)} async-done(((bf16[32,16,512]{2,1,0:T(8,128)(2,1)}), bf16[32,16,512]{2,1,0:T(8,128)(2,1)S(1)}, u32[]{:S(2)}, u32[]{:S(2)}) %all-to-all-start.3) | async-done | bytes 524320 | tf_op jit(solution)/shard_map/all_to_all | solution.py:69
  339.5 0.9 convolution_convert_fusion.4
  (31 shorter events, 1.8 us)
Async XLA Ops:
  7.2 146.7 %copy-start = (bf16[1,4096,256]{2,1,0:T(8,128)(2,1)S(1)}, bf16[1,4096,256]{2,1,0:T(8,128)(2,1)}, u32[]{:S(2)}) copy-start(bf16[1,4096,256]{2,1,0:T(8,128)(2,1)} %param.10) | copy-start | bytes 6291460
  7.2 30.1 %all-gather.5.cloned.1.call-start = ((), (), s32[]{:S(2)}) async-start(), calls=%async_computation.7 | async-start | bytes 1179648 | tf_op jit(solution)/shard_map/all_gather | solution.py:38
  12.2 29.5 %all-to-all-start = ((bf16[32,16,1]{1,2,0:T(2,128)(2,1)}), bf16[32,16,1]{1,2,0:T(2,128)(2,1)S(1)}, u32[]{:S(2)}, u32[]{:S(2)}) async-start(bf16[32,16,1]{1,2,0:T(2,128)(2,1)} %copy.51), calls=%async_computation | async-start | bytes 32768 | tf_op jit(solution)/shard_map/all_to_all | solution.py:46
  41.6 106.2 %all-to-all-start.2 = ((bf16[32,16,4096]{2,1,0:T(8,128)(2,1)}), bf16[32,16,4096]{2,1,0:T(8,128)(2,1)}, u32[]{:S(2)}, u32[]{:S(2)}) async-start(bf16[32,16,4096]{2,1,0:T(8,128)(2,1)} %bitcast.63), calls=%async_computation.2 | async-start | bytes 8388608 | tf_op jit(solution)/shard_map/all_to_all | solution.py:44
  51.5 28.3 %all-gather.3.cloned.1.call-start = ((), (), s32[]{:S(2)}) async-start(), calls=%async_computation.6 | async-start | bytes 1179648 | tf_op jit(solution)/shard_map/all_gather | solution.py:39
  147.8 100.2 %all-to-all-start.1 = ((bf16[32,16,4096]{2,1,0:T(8,128)(2,1)}), bf16[32,16,4096]{2,1,0:T(8,128)(2,1)}, u32[]{:S(2)}, u32[]{:S(2)}) async-start(bf16[32,16,4096]{2,1,0:T(8,128)(2,1)} %bitcast.64), calls=%async_computation.1 | async-start | bytes 8388608 | tf_op jit(solution)/shard_map/all_to_all | solution.py:45
  153.7 155.5 %reduce-scatter.2.cloned.1.call-start = ((), (), s32[]{:S(2)}) async-start(), calls=%async_computation.8 | async-start | bytes 9437184 | tf_op jit(solution)/shard_map/reduce_scatter | solution.py:64
  252.2 0.8 copy-start.1
  269.6 41.7 %all-to-all-start.4 = ((bf16[32,16,1]{1,2,0:T(2,128)(2,1)}), bf16[32,16,1]{1,2,0:T(2,128)(2,1)S(1)}, u32[]{:S(2)}, u32[]{:S(2)}) async-start(bf16[32,16,1]{1,2,0:T(2,128)(2,1)} %all_to_all.46), calls=%async_computation.5 | async-start | bytes 32768 | tf_op jit(solution)/shard_map/all_to_all | solution.py:70
  311.3 28.2 %all-to-all-start.3 = ((bf16[32,16,512]{2,1,0:T(8,128)(2,1)}), bf16[32,16,512]{2,1,0:T(8,128)(2,1)S(1)}, u32[]{:S(2)}, u32[]{:S(2)}) async-start(bf16[32,16,512]{2,1,0:T(8,128)(2,1)} %bitcast.9), calls=%async_computation.4 | async-start | bytes 1048576 | tf_op jit(solution)/shard_map/all_to_all | solution.py:69
  321.6 4.9 %copy-start.2 = (f32[512,256]{0,1:T(8,128)S(1)}, f32[512,256]{0,1:T(8,128)}, u32[]{:S(2)}) copy-start(f32[512,256]{0,1:T(8,128)} %copy-done.1) | copy-start | bytes 1572868
Sparse Core Ops, SparseCore 0:
  9.9 27.3 all-gather.4
  54.2 25.5 all-gather.2
  257.8 51.3 reduce-scatter.1
where the time goes:
time: 348 us; the launch traced here: 347 us
  waiting for transfers between devices  235 us (68%)
  starting transfers between devices  45.2 us (13%)
  matrix products  32.7 us (9%)
  between operations  13.9 us (4%)
  blocking collectives  11.2 us (3%)
  local copies, waits for them, and re-layouts  4.86 us (1%)
  other arithmetic  4.23 us (1%)
    all_to_all x1, waiting for transfers between devices, shards(): lax.all_to_all(dy_send, 'exp', split_axis=0, concat_axis=0, tiled=True)  90.6 us
    all_to_all x1, waiting for transfers between devices, shards(): lax.all_to_all(x_send, 'exp', split_axis=0, concat_axis=0, tiled=True)  63.6 us
    reduce_scatter x1, waiting for transfers between devices, shards(): lax.psum_scatter(row_terms, 'head', scatter_dimension=1, tiled=True)  32 us
    all_gather x1, waiting for transfers between devices, shards(): lax.all_gather(cotangent, 'head', axis=1, tiled=True)  27.6 us
    all_gather x1, waiting for transfers between devices, shards(): lax.all_gather(tokens, 'head', axis=1, tiled=True)  12.6 us
    all_to_all x1, starting transfers between devices, shards(): lax.all_to_all(gate_send, 'exp', split_axis=0, concat_axis=0, tiled=True)  11.5 us
    psum x1, blocking collectives, shards(): score = lax.psum(score_part, 'head').astype(jnp.bfloat16)  11.2 us
    dot_general x4, matrix products, contract_rows(): lax.dot_general(left, right, (((0,), (0,)), ((), ())), preferred_element_...  11 us
  transfers between devices with their start and end apart: 8, of which 6 were waited for; matrix products, arithmetic and copies ran while one was open for 9% of the time, Pallas kernels for 0%

commit v1 on v0

v1 whole, which is shorter than its diff:
```python
import math

import jax
import jax.numpy as jnp
from jax import lax
from jax.experimental import pallas as pl
from jax.experimental.pallas import tpu as pltpu
from jax.sharding import PartitionSpec as P

MESH = pl.DeviceIdType.MESH
BF16, F32, I32 = jnp.bfloat16, jnp.float32, jnp.int32

NZ, NY, NX = 8, 4, 4
EXP, HEAD = NZ * NY, 2 * NX
CAP = 16
TOK = 128
CH = NZ * CAP
NCH = NY
ROWS = NCH * CH
FL = 512
HID = 256
D = HEAD * FL
XD = 2 * FL
MSG = XD + 128
RET = FL + 128


def gelu_parts(pre):
    phi = 0.5 * (1.0 + lax.erf(pre * math.sqrt(0.5)))
    act = pre * phi
    slope = phi + pre * jnp.exp(-0.5 * pre * pre) * (1.0 / math.sqrt(2.0 * math.pi))
    return act, slope


def nn(a, b):
    return jnp.dot(a, b, preferred_element_type=F32)


def nt(a, b):
    return lax.dot_general(a, b, (((1,), (1,)), ((), ())), preferred_element_type=F32)


def tn(a, b):
    return lax.dot_general(a, b, (((0,), (0,)), ((), ())), preferred_element_type=F32)


def kernel(
    tok_ref, cot_ref, gates_ref, ids_ref, wup_hbm, wdn_hbm,
    gt_out, gg_out, gup_out, gdn_out,
    wup, wdn, gup, gdn, pt0, pt1, send, rows, scaled, delta,
    sib_send, sib_recv, own, m1s, m1r, m2s, m2r, sc_send, sc_recv, ret_send, ret_recv,
    w_sem, o_sem,
    d_send, d_recv, ga_send, ga_recv, gb_send, gb_recv, a2_send, a2_recv, b2_send, b2_recv,
    gs_send, gs_recv, sib_ss, sib_rs, m1_ss, m1_rs, m2_ss, m2_rs, sc_ss, sc_rs, r_ss, r_rs,
):
    e, h = lax.axis_index("exp"), lax.axis_index("head")
    z, y = e // NY, lax.rem(e, NY)
    x, c = h // 2, lax.rem(h, 2)

    def head_of(xx, cc):
        return lax.rem(xx + NX, NX) * 2 + cc

    right, left, opp = head_of(x + 1, c), head_of(x - 1, c), head_of(x + 2, c)
    sib = x * 2 + (1 - c)

    def exp_of(zz, yy):
        return lax.rem(zz + NZ, NZ) * NY + lax.rem(yy + NY, NY)

    barrier = pltpu.get_barrier_semaphore()

    def greet_exp(i, carry):
        pl.semaphore_signal(barrier, inc=1, device_id=(lax.rem(e + i, EXP), h), device_id_type=MESH)
        return carry

    def greet_head(i, carry):
        pl.semaphore_signal(barrier, inc=1, device_id=(e, lax.rem(h + i, HEAD)), device_id_type=MESH)
        return carry

    lax.fori_loop(1, EXP, greet_exp, 0)
    lax.fori_loop(1, HEAD, greet_head, 0)

    load_up = pltpu.make_async_copy(wup_hbm.at[0], wup, w_sem.at[0])
    load_dn = pltpu.make_async_copy(wdn_hbm.at[0], wdn, w_sem.at[1])
    load_up.start()
    load_dn.start()

    ids = ids_ref[...]

    def offset_of(expert):
        return ((y - (expert & (NY - 1))) & (NY - 1)) * NZ + ((z - (expert >> 2)) & (NZ - 1))

    r0, r1 = offset_of(ids[:, 0:1]), offset_of(ids[:, 1:2])
    lane = lax.broadcasted_iota(I32, (TOK, 128), 1)
    sub = lax.broadcasted_iota(I32, (TOK, 128), 0)
    oh0, oh1 = (r0 == lane).astype(F32), (r1 == lane).astype(F32)
    before = nn((lane < sub).astype(BF16), (oh0 + oh1).astype(BF16))
    d0 = r0 * CAP + jnp.sum(oh0 * before, axis=1, keepdims=True).astype(I32)
    d1 = r1 * CAP + jnp.sum(oh1 * before, axis=1, keepdims=True).astype(I32)
    slots = lax.broadcasted_iota(I32, (TOK, ROWS), 1)
    pt0[...] = (d0 == slots).astype(BF16)
    pt1[...] = (d1 == slots).astype(BF16)
    gates = gates_ref[...].astype(F32)
    gate0 = jnp.broadcast_to(gates[:, 0:1], (TOK, 128)).astype(BF16)
    gate1 = jnp.broadcast_to(gates[:, 1:2], (TOK, 128)).astype(BF16)

    def rows_of(k):
        return pl.ds(k * CH, CH)

    def block(p):
        return pl.ds(pl.multiple_of(p * CAP, CAP), CAP)

    def fill(k):
        here = rows_of(k)
        p0, p1 = pt0[:, here], pt1[:, here]
        both = p0 + p1
        send[here, 0:FL] = tn(both, tok_ref[...]).astype(BF16)
        send[here, FL:XD] = tn(both, cot_ref[...]).astype(BF16)
        send[here, XD:MSG] = (tn(p0, gate0) + tn(p1, gate1)).astype(BF16)

    def remote(src, dst, ss, rs, exp_i, head_i):
        return pltpu.make_async_remote_copy(
            src_ref=src, dst_ref=dst, send_sem=ss, recv_sem=rs,
            device_id=(exp_i, head_i), device_id_type=MESH,
        )

    def dispatch(k):
        def one(j, carry):
            p = k * NZ + j
            remote(
                send.at[block(p)], rows.at[h, block(p)], d_send.at[0], d_recv.at[k],
                exp_of(z - j, y - k), h,
            ).start()
            return carry

        lax.fori_loop(1 if k == 0 else 0, NZ, one, 0)

    def wait_recv(ref, rs):
        remote(ref, ref, rs, rs, e, sib).wait_recv()

    def wait_send(ref, ss):
        remote(ref, ref, ss, ss, e, sib).wait_send()

    fill(0)
    pl.semaphore_wait(barrier, EXP - 1 + HEAD - 1)
    dispatch(0)
    rows[h, 0:CAP, :] = send[0:CAP, :]
    for k in range(1, NCH):
        fill(k)
        dispatch(k)

    def part(hh, k, start=0, size=CH):
        return rows.at[hh, pl.ds(k * CH + start, size), pl.ds(0, XD)]

    half = CH // 2

    def gather1(k):
        if k == 0:
            wait_recv(rows.at[h, pl.ds(CAP, CH - CAP)], d_recv.at[k])
        else:
            wait_recv(rows.at[h, rows_of(k)], d_recv.at[k])
        mine = part(h, k)
        remote(mine, mine, ga_send.at[0], ga_recv.at[k], e, right).start()
        remote(mine, mine, gb_send.at[0], gb_recv.at[k], e, left).start()
        remote(mine, mine, gs_send.at[0], gs_recv.at[k, 0], e, sib).start()

    def gather2(k):
        low, high = part(left, k, 0, half), part(right, k, half, half)
        wait_recv(part(left, k), ga_recv.at[k])
        remote(low, low, a2_send.at[0], a2_recv.at[k], e, right).start()
        remote(part(left, k), part(left, k), gs_send.at[1], gs_recv.at[k, 1], e, sib).start()
        wait_recv(part(right, k), gb_recv.at[k])
        remote(high, high, b2_send.at[0], b2_recv.at[k], e, left).start()
        remote(part(right, k), part(right, k), gs_send.at[2], gs_recv.at[k, 2], e, sib).start()

    def gather3(k):
        wait_recv(part(opp, k, 0, half), a2_recv.at[k])
        wait_recv(part(opp, k, half, half), b2_recv.at[k])
        remote(part(opp, k), part(opp, k), gs_send.at[3], gs_recv.at[k, 3], e, sib).start()

    def gather4(k):
        for i in range(4):
            wait_recv(part(h, k), gs_recv.at[k, i])

    eye = lax.broadcasted_iota(I32, (CH, CH), 0) == lax.broadcasted_iota(I32, (CH, CH), 1)

    def features(hh):
        return pl.ds(pl.multiple_of(hh * FL, FL), FL)

    def compute(k):
        here = rows_of(k)

        def step(hh, sums):
            pre, back = sums
            pre = pre + nn(rows[hh, here, 0:FL], wup[features(hh), :])
            back = back + nt(rows[hh, here, FL:XD], wdn[:, features(hh)])
            return pre, back

        zero = jnp.zeros((CH, HID), F32)
        pre, back = lax.fori_loop(0, HEAD, step, (zero, zero))
        g = rows[h, here, XD:MSG][:, 0:1].astype(F32)
        act, slope = gelu_parts(pre)
        score = jnp.sum(back * act, axis=1, keepdims=True)
        scaled[here, :] = (g * act).astype(BF16)
        delta[here, :] = (g * back * slope).astype(BF16)

        def give(xx, carry):
            sib_send[k, xx] = nt(delta[here, :], wup[features(xx * 2 + (1 - c)), :]).astype(BF16)
            return carry

        lax.fori_loop(0, NX, give, 0)
        remote(sib_send.at[k], sib_recv.at[k], sib_ss.at[k], sib_rs.at[k], e, sib).start()
        line = jnp.sum(jnp.where(eye, score, 0.0), axis=0, keepdims=True)
        sc_send[k] = line
        sc_recv[k, h] = line

        def tell(i, carry):
            remote(
                sc_send.at[k], sc_recv.at[k, h], sc_ss.at[k], sc_rs.at[k], e, lax.rem(h + i, HEAD)
            ).start()
            return carry

        lax.fori_loop(1, HEAD, tell, 0)

        def keep(xx, carry):
            own[k, xx] = nt(delta[here, :], wup[features(xx * 2 + c), :])
            return carry

        lax.fori_loop(0, NX, keep, 0)

    def pair(k, xx, start, size):
        at = lax.rem(xx + NX, NX)
        cols = pl.ds(start, size)
        return own[k, at, :, cols] + sib_recv[k, at, :, cols].astype(F32)

    hf = FL // 2

    def reduce1(k):
        wait_recv(sib_recv.at[k], sib_rs.at[k])
        m1s[k, 0] = pair(k, x + 2, 0, hf).astype(BF16)
        remote(m1s.at[k, 0], m1r.at[k, 0], m1_ss.at[k, 0], m1_rs.at[k, 0], e, right).start()
        m1s[k, 1] = pair(k, x + 2, hf, hf).astype(BF16)
        remote(m1s.at[k, 1], m1r.at[k, 1], m1_ss.at[k, 1], m1_rs.at[k, 1], e, left).start()

    def reduce2(k):
        m2s[k, 0, :, hf:FL] = pair(k, x + 1, hf, hf).astype(BF16)
        m2s[k, 1, :, 0:hf] = pair(k, x - 1, 0, hf).astype(BF16)
        wait_recv(m1r.at[k, 0], m1_rs.at[k, 0])
        m2s[k, 0, :, 0:hf] = (pair(k, x + 1, 0, hf) + m1r[k, 0].astype(F32)).astype(BF16)
        remote(m2s.at[k, 0], m2r.at[k, 0], m2_ss.at[k, 0], m2_rs.at[k, 0], e, right).start()
        wait_recv(m1r.at[k, 1], m1_rs.at[k, 1])
        m2s[k, 1, :, hf:FL] = (pair(k, x - 1, hf, hf) + m1r[k, 1].astype(F32)).astype(BF16)
        remote(m2s.at[k, 1], m2r.at[k, 1], m2_ss.at[k, 1], m2_rs.at[k, 1], e, left).start()

    def reduce3(k):
        here = rows_of(k)
        wait_recv(sc_recv.at[k, pl.ds(0, HEAD - 1)], sc_rs.at[k])
        total = sc_recv[k, 0]
        for i in range(1, HEAD):
            total = total + sc_recv[k, i]
        column = jnp.sum(jnp.where(eye, total, 0.0), axis=1, keepdims=True)
        ret_send[here, FL:RET] = jnp.broadcast_to(column, (CH, 128)).astype(BF16)
        wait_recv(m2r.at[k, 0], m2_rs.at[k, 0])
        wait_recv(m2r.at[k, 1], m2_rs.at[k, 1])
        done = pair(k, x, 0, FL) + m2r[k, 0].astype(F32) + m2r[k, 1].astype(F32)
        ret_send[here, 0:FL] = done.astype(BF16)

        def one(j, carry):
            p = k * NZ + j
            remote(
                ret_send.at[block(p)], ret_recv.at[block(p)], r_ss.at[0], r_rs.at[k],
                exp_of(z + j, y + k), h,
            ).start()
            return carry

        lax.fori_loop(1 if k == 0 else 0, NZ, one, 0)
        if k == 0:
            ret_recv[0:CAP, :] = ret_send[0:CAP, :]

    def weights_down():
        def step(hh, carry):
            gdn[:, features(hh)] = tn(scaled[...], rows[hh, :, FL:XD]).astype(BF16)
            return carry

        lax.fori_loop(0, HEAD, step, 0)
        pltpu.make_async_copy(gdn, gdn_out.at[0], o_sem.at[1]).start()

    def weights_up():
        def step(hh, carry):
            gup[features(hh), :] = tn(rows[hh, :, 0:FL], delta[...]).astype(BF16)
            return carry

        lax.fori_loop(0, HEAD, step, 0)
        pltpu.make_async_copy(gup, gup_out.at[0], o_sem.at[0]).start()

    gather1(0)
    gather1(1)
    gather2(0)
    gather1(2)
    gather2(1)
    gather3(0)
    gather1(3)
    gather2(2)
    gather3(1)
    gather4(0)
    load_up.wait()
    load_dn.wait()
    compute(0)
    gather2(3)
    gather3(2)
    reduce1(0)
    gather4(1)
    compute(1)
    reduce2(0)
    gather3(3)
    reduce1(1)
    gather4(2)
    compute(2)
    reduce3(0)
    reduce2(1)
    reduce1(2)
    gather4(3)
    compute(3)
    reduce3(1)
    reduce2(2)
    reduce1(3)
    weights_down()
    reduce3(2)
    reduce2(3)
    weights_up()
    reduce3(3)

    back0 = jnp.zeros((TOK, RET), F32)
    back1 = jnp.zeros((TOK, RET), F32)
    for k in range(NCH):
        if k == 0:
            wait_recv(ret_recv.at[pl.ds(CAP, CH - CAP)], r_rs.at[k])
        else:
            wait_recv(ret_recv.at[rows_of(k)], r_rs.at[k])
        back0 = back0 + nn(pt0[:, rows_of(k)], ret_recv[rows_of(k), :])
        back1 = back1 + nn(pt1[:, rows_of(k)], ret_recv[rows_of(k), :])
    gt_out[...] = (back0[:, 0:FL] + back1[:, 0:FL]).astype(BF16)
    gg_out[:, 0:1] = back0[:, FL:FL + 1].astype(BF16)
    gg_out[:, 1:2] = back1[:, FL:FL + 1].astype(BF16)

    wait_send(send.at[pl.ds(CAP, ROWS - CAP)], d_send.at[0])
    whole = rows.at[0, :, pl.ds(0, XD)]
    wait_send(whole, ga_send.at[0])
    wait_send(whole, gb_send.at[0])
    for i in range(4):
        wait_send(whole, gs_send.at[i])
    halves = rows.at[0, pl.ds(0, ROWS // 2), pl.ds(0, XD)]
    wait_send(halves, a2_send.at[0])
    wait_send(halves, b2_send.at[0])
    for k in range(NCH):
        wait_send(sib_send.at[k], sib_ss.at[k])
        for i in range(2):
            wait_send(m1s.at[k, i], m1_ss.at[k, i])
            wait_send(m2s.at[k, i], m2_ss.at[k, i])
        wait_send(sc_recv.at[k, pl.ds(0, HEAD - 1)], sc_ss.at[k])
    wait_send(ret_send.at[pl.ds(CAP, ROWS - CAP)], r_ss.at[0])
    pltpu.make_async_copy(gdn, gdn_out.at[0], o_sem.at[1]).wait()
    pltpu.make_async_copy(gup, gup_out.at[0], o_sem.at[0]).wait()


def shards(tokens, cotangent, gates, expert_ids, w_up, w_down):
    vmem = pl.BlockSpec(memory_space=pltpu.VMEM)
    hbm = pl.BlockSpec(memory_space=pl.ANY)
    dma = pltpu.SemaphoreType.DMA
    return pl.pallas_call(
        kernel,
        out_shape=(
            jax.ShapeDtypeStruct((TOK, FL), BF16),
            jax.ShapeDtypeStruct((TOK, 2), BF16),
            jax.ShapeDtypeStruct((1, D, HID), BF16),
            jax.ShapeDtypeStruct((1, HID, D), BF16),
        ),
        in_specs=[vmem, vmem, vmem, vmem, hbm, hbm],
        out_specs=(vmem, vmem, hbm, hbm),
        scratch_shapes=[
            pltpu.VMEM((D, HID), BF16),
            pltpu.VMEM((HID, D), BF16),
            pltpu.VMEM((D, HID), BF16),
            pltpu.VMEM((HID, D), BF16),
            pltpu.VMEM((TOK, ROWS), BF16),
            pltpu.VMEM((TOK, ROWS), BF16),
            pltpu.VMEM((ROWS, MSG), BF16),
            pltpu.VMEM((HEAD, ROWS, MSG), BF16),
            pltpu.VMEM((ROWS, HID), BF16),
            pltpu.VMEM((ROWS, HID), BF16),
            pltpu.VMEM((NCH, NX, CH, FL), BF16),
            pltpu.VMEM((NCH, NX, CH, FL), BF16),
            pltpu.VMEM((NCH, NX, CH, FL), F32),
            pltpu.VMEM((NCH, 2, CH, FL // 2), BF16),
            pltpu.VMEM((NCH, 2, CH, FL // 2), BF16),
            pltpu.VMEM((NCH, 2, CH, FL), BF16),
            pltpu.VMEM((NCH, 2, CH, FL), BF16),
            pltpu.VMEM((NCH, 1, CH), F32),
            pltpu.VMEM((NCH, HEAD, 1, CH), F32),
            pltpu.VMEM((ROWS, RET), BF16),
            pltpu.VMEM((ROWS, RET), BF16),
            dma((2,)),
            dma((2,)),
            dma((1,)), dma((NCH,)),
            dma((1,)), dma((NCH,)),
            dma((1,)), dma((NCH,)),
            dma((1,)), dma((NCH,)),
            dma((1,)), dma((NCH,)),
            dma((4,)), dma((NCH, 4)),
            dma((NCH,)), dma((NCH,)),
            dma((NCH, 2)), dma((NCH, 2)),
            dma((NCH, 2)), dma((NCH, 2)),
            dma((NCH,)), dma((NCH,)),
            dma((1,)), dma((NCH,)),
        ],
        compiler_params=pltpu.CompilerParams(
            collective_id=0, has_side_effects=True, vmem_limit_bytes=56 * 1024 * 1024
        ),
        cost_estimate=pl.CostEstimate(
            flops=10 * ROWS * D * HID, bytes_accessed=8 * D * HID, transcendentals=2 * ROWS * HID
        ),
    )(tokens, cotangent, gates, expert_ids, w_up, w_down)


def solution(mesh):
    return jax.shard_map(
        shards,
        mesh=mesh,
        in_specs=(
            P("exp", "head"),
            P("exp", "head"),
            P("exp", None),
            P("exp", None),
            P("exp", None, "head"),
            P("exp", "head", None),
        ),
        out_specs=(
            P("exp", "head"),
            P("exp", None),
            P("exp", None, "head"),
            P("exp", "head", None),
        ),
        check_vma=False,
    )
```

time: 348 us -> 102 us (0.29)
  waiting for transfers between devices: 235 us -> 0 us
  Pallas kernels: 0 us -> 90.9 us
  starting transfers between devices: 45.2 us -> 0 us
  matrix products: 32.7 us -> 0 us
  between operations: 13.9 us -> 0.64 us
  blocking collectives: 11.2 us -> 0 us
  local copies, waits for them, and re-layouts: 4.86 us -> 10.2 us
  other arithmetic: 4.23 us -> 0 us
    all_to_all x5 -> x0, waiting for transfers between devices: 161 us -> none  [the longest x1 90.6 us: shards(): lax.all_to_all(dy_send, 'exp', split_axis=0, concat_axis=0, tiled=True)]
    pallas_call x0 -> x1, Pallas kernels: none -> 90.9 us  [shards(): pl.pallas_call(kernel, out_shape=(jax.ShapeDtypeStruct((TOK, FL), BF16),...]
    all_to_all x5 -> x0, starting transfers between devices: 45.1 us -> none  [the longest x1 11.5 us: shards(): lax.all_to_all(gate_send, 'exp', split_axis=0, concat_axis=0, tiled=True)]
    all_gather x2 -> x0, waiting for transfers between devices: 40.2 us -> none  [the longest x1 27.6 us: shards(): lax.all_gather(cotangent, 'head', axis=1, tiled=True)]
    dot_general x10 -> x0, matrix products: 32.7 us -> none  [the longest x4 11 us: contract_rows(): lax.dot_general(left, right, (((0,), (0,)), ((), ())), preferred_element_...]
    reduce_scatter x1 -> x0, waiting for transfers between devices: 32 us -> none  [shards(): lax.psum_scatter(row_terms, 'head', scatter_dimension=1, tiled=True)]
    psum x1 -> x0, blocking collectives: 11.2 us -> none  [shards(): score = lax.psum(score_part, 'head').astype(jnp.bfloat16)]
    unnamed x8 -> x7, local copies, waits for them, and re-layouts: 2.38 us -> 8.88 us
  transfers between devices with their start and end apart: 8 -> 0, of which waited for: 6 -> 0; matrix products, arithmetic and copies ran while one was open for 9% -> 0% of each run, Pallas kernels for 0% -> 0%
where the time goes in v1:
time: 102 us
  Pallas kernels  90.9 us (89%)
  local copies, waits for them, and re-layouts  10.2 us (10%)
    pallas_call x1, Pallas kernels, shards(): pl.pallas_call(kernel, out_shape=(jax.ShapeDtypeStruct((TOK, FL), BF16),...  90.9 us
    unnamed x7, local copies, waits for them, and re-layouts  8.88 us

profile of v1, /device:TPU:2, one launch (start us, length us, event | category | flops | bytes accessed | tf_op | source)
XLA Modules:
  0.0 101.8 jit_solution(17021036322176312035)
XLA Ops:
  0.6 1.4 %copy.10.gates_ref = bf16[128,2]{1,0:T(8,128)(2,1)} copy(bf16[128,2]{0,1:T(2,128)(2,1)} %param.8) | data formatting | bytes 1024 | tf_op args[2]
  2.0 1.4 %copy.11.ids_ref = s32[128,2]{1,0:T(8,128)} copy(s32[128,2]{0,1:T(2,128)} %param.9) | data formatting | bytes 2048 | tf_op args[3]
  3.4 90.9 %shard_map.93 = (bf16[128,512]{1,0:T(8,128)(2,1)}, bf16[128,2]{1,0:T(8,128)(2,1)}, bf16[1,4096,256]{2,1,0:T(8,128)(2,1)}, bf16[1,256,4096]{2,1,0:T(8,128)(2,1)}) custom-call(bf16[128,512]{1,0:T(8,128)(2,1)} %tok_ref.1, bf16[128,512]{1,0:T(8,128)(2,1)} %cot_ref.1, bf16[128,2]{1,0:T(8,128)(2,1)} %copy.10.gates_ref, s32[128,2]{1,0:T(8,128)} %copy.11.ids_ref, ...), custom_call_target="tpu_custom_call" | custom-call | flops 5368709120 | bytes 8388608 | tf_op jit(solution)/shard_map/pallas_call | solution.py:369
  94.3 1.4 %copy.12 = bf16[128,2]{0,1:T(2,128)(2,1)} copy(bf16[128,2]{1,0:T(8,128)(2,1)} %get-tuple-element.5) | data formatting | bytes 1024 | tf_op jit(solution)/shard_map/pallas_call | solution.py:369
  95.7 1.6 %copy.16 = bf16[128,512]{1,0:T(8,128)(2,1)} copy(bf16[128,512]{1,0:T(8,128)(2,1)} %get-tuple-element.12) | data formatting | bytes 262144
  97.3 0.0 copy-start
  97.3 3.2 %copy.17 = bf16[1,4096,256]{2,1,0:T(8,128)(2,1)} copy(bf16[1,4096,256]{2,1,0:T(8,128)(2,1)} %get-tuple-element.14) | data formatting | bytes 4194304
  100.5 0.0 copy-done
  100.5 1.3 %copy.18 = bf16[1,256,4096]{2,1,0:T(8,128)(2,1)} copy(bf16[1,256,4096]{2,1,0:T(8,128)(2,1)S(1)} %copy-done) | data formatting | bytes 4194304
Async XLA Ops:
  97.3 3.2 %copy-start = (bf16[1,256,4096]{2,1,0:T(8,128)(2,1)S(1)}, bf16[1,256,4096]{2,1,0:T(8,128)(2,1)}, u32[]{:S(2)}) copy-start(bf16[1,256,4096]{2,1,0:T(8,128)(2,1)} %get-tuple-element.15) | copy-start | bytes 6291460

commit v2 on v1

--- a/solution.py
+++ b/solution.py
@@ -14,8 +14,9 @@
 EXP, HEAD = NZ * NY, 2 * NX
 CAP = 16
 TOK = 128
-CH = NZ * CAP
-NCH = NY
+PER = 4
+CH = PER * CAP
+NCH = EXP // PER
 ROWS = NCH * CH
 FL = 512
 HID = 256
@@ -25,6 +26,21 @@
 RET = FL + 128
 
 
+def offsets():
+    order = []
+    for reach, late in ((0, 0), (1, 0), (2, 0), (3, 0), (4, 0), (3, 1), (2, 1), (1, 1)):
+        if reach in (0, NZ // 2):
+            order += [(reach, 0), (reach, 1), (reach, NY - 1), (reach, 2)]
+        elif late:
+            order += [(reach, NY - 1), (NZ - reach, 1), (reach, 2), (NZ - reach, 2)]
+        else:
+            order += [(reach, 0), (NZ - reach, 0), (reach, 1), (NZ - reach, NY - 1)]
+    return order
+
+
+ORDER = offsets()
+
+
 def gelu_parts(pre):
     phi = 0.5 * (1.0 + lax.erf(pre * math.sqrt(0.5)))
     act = pre * phi
@@ -46,10 +62,10 @@
 
 def kernel(
     tok_ref, cot_ref, gates_ref, ids_ref, wup_hbm, wdn_hbm,
-    gt_out, gg_out, gup_out, gdn_out,
-    wup, wdn, gup, gdn, pt0, pt1, send, rows, scaled, delta,
+    gt_out, gg_out, gup, gdn,
+    wup, wdn, wup_t, wdn_t, pt0, pt1, send, rows, scaled, delta,
     sib_send, sib_recv, own, m1s, m1r, m2s, m2r, sc_send, sc_recv, ret_send, ret_recv,
-    w_sem, o_sem,
+    w_sem,
     d_send, d_recv, ga_send, ga_recv, gb_send, gb_recv, a2_send, a2_recv, b2_send, b2_recv,
     gs_send, gs_recv, sib_ss, sib_rs, m1_ss, m1_rs, m2_ss, m2_rs, sc_ss, sc_rs, r_ss, r_rs,
 ):
@@ -84,30 +100,36 @@
     load_up.start()
     load_dn.start()
 
-    ids = ids_ref[...]
-
-    def offset_of(expert):
-        return ((y - (expert & (NY - 1))) & (NY - 1)) * NZ + ((z - (expert >> 2)) & (NZ - 1))
-
-    r0, r1 = offset_of(ids[:, 0:1]), offset_of(ids[:, 1:2])
     lane = lax.broadcasted_iota(I32, (TOK, 128), 1)
     sub = lax.broadcasted_iota(I32, (TOK, 128), 0)
-    oh0, oh1 = (r0 == lane).astype(F32), (r1 == lane).astype(F32)
-    before = nn((lane < sub).astype(BF16), (oh0 + oh1).astype(BF16))
-    d0 = r0 * CAP + jnp.sum(oh0 * before, axis=1, keepdims=True).astype(I32)
-    d1 = r1 * CAP + jnp.sum(oh1 * before, axis=1, keepdims=True).astype(I32)
+
+    def column(ref, k):
+        line = ref[k:k + 1, :].astype(F32)
+        return jnp.sum(jnp.where(lane == sub, line, 0.0), axis=1, keepdims=True)
+
+    def offset_of(expert):
+        return ((z - (expert >> 2)) & (NZ - 1)) * NY + ((y - (expert & (NY - 1))) & (NY - 1))
+
+    r0, r1 = offset_of(column(ids_ref, 0).astype(I32)), offset_of(column(ids_ref, 1).astype(I32))
+    first = jnp.zeros((1, 128), F32)
+    for p, (dz, dy) in enumerate(ORDER):
+        first = jnp.where(lane[0:1] == dz * NY + dy, float(p * CAP), first)
+    oh0, oh1 = r0 == lane, r1 == lane
+    both = (oh0 | oh1).astype(BF16)
+    place = nn((lane < sub).astype(BF16), both) + first
+    d0 = jnp.sum(jnp.where(oh0, place, 0.0), axis=1, keepdims=True).astype(I32)
+    d1 = jnp.sum(jnp.where(oh1, place, 0.0), axis=1, keepdims=True).astype(I32)
     slots = lax.broadcasted_iota(I32, (TOK, ROWS), 1)
     pt0[...] = (d0 == slots).astype(BF16)
     pt1[...] = (d1 == slots).astype(BF16)
-    gates = gates_ref[...].astype(F32)
-    gate0 = jnp.broadcast_to(gates[:, 0:1], (TOK, 128)).astype(BF16)
-    gate1 = jnp.broadcast_to(gates[:, 1:2], (TOK, 128)).astype(BF16)
+    gate0 = jnp.broadcast_to(column(gates_ref, 0), (TOK, 128)).astype(BF16)
+    gate1 = jnp.broadcast_to(column(gates_ref, 1), (TOK, 128)).astype(BF16)
 
     def rows_of(k):
         return pl.ds(k * CH, CH)
 
     def block(p):
-        return pl.ds(pl.multiple_of(p * CAP, CAP), CAP)
+        return pl.ds(p * CAP, CAP)
 
     def fill(k):
         here = rows_of(k)
@@ -124,15 +146,12 @@
         )
 
     def dispatch(k):
-        def one(j, carry):
-            p = k * NZ + j
+        for p in range(max(k * PER, 1), (k + 1) * PER):
+            dz, dy = ORDER[p]
             remote(
                 send.at[block(p)], rows.at[h, block(p)], d_send.at[0], d_recv.at[k],
-                exp_of(z - j, y - k), h,
+                exp_of(z - dz, y - dy), h,
             ).start()
-            return carry
-
-        lax.fori_loop(1 if k == 0 else 0, NZ, one, 0)
 
     def wait_recv(ref, rs):
         remote(ref, ref, rs, rs, e, sib).wait_recv()
@@ -147,6 +166,12 @@
     for k in range(1, NCH):
         fill(k)
         dispatch(k)
+    load_up.wait()
+    load_dn.wait()
+    for hh in range(HEAD):
+        part_of = pl.ds(hh * FL, FL)
+        wup_t[:, part_of] = wup[part_of, :].T
+        wdn_t[part_of, :] = wdn[:, part_of].T
 
     def part(hh, k, start=0, size=CH):
         return rows.at[hh, pl.ds(k * CH + start, size), pl.ds(0, XD)]
@@ -181,7 +206,7 @@
         for i in range(4):
             wait_recv(part(h, k), gs_recv.at[k, i])
 
-    eye = lax.broadcasted_iota(I32, (CH, CH), 0) == lax.broadcasted_iota(I32, (CH, CH), 1)
+    eye = lane[0:CH] == sub[0:CH]
 
     def features(hh):
         return pl.ds(pl.multiple_of(hh * FL, FL), FL)
@@ -189,25 +214,21 @@
     def compute(k):
         here = rows_of(k)
 
-        def step(hh, sums):
-            pre, back = sums
-            pre = pre + nn(rows[hh, here, 0:FL], wup[features(hh), :])
-            back = back + nt(rows[hh, here, FL:XD], wdn[:, features(hh)])
-            return pre, back
-
-        zero = jnp.zeros((CH, HID), F32)
-        pre, back = lax.fori_loop(0, HEAD, step, (zero, zero))
+        pre = jnp.zeros((CH, HID), F32)
+        back = jnp.zeros((CH, HID), F32)
+        for hh in range(HEAD):
+            part_of = pl.ds(hh * FL, FL)
+            pre = pre + nn(rows[hh, here, 0:FL], wup[part_of, :])
+            back = back + nn(rows[hh, here, FL:XD], wdn_t[part_of, :])
         g = rows[h, here, XD:MSG][:, 0:1].astype(F32)
         act, slope = gelu_parts(pre)
         score = jnp.sum(back * act, axis=1, keepdims=True)
         scaled[here, :] = (g * act).astype(BF16)
         delta[here, :] = (g * back * slope).astype(BF16)
 
-        def give(xx, carry):
-            sib_send[k, xx] = nt(delta[here, :], wup[features(xx * 2 + (1 - c)), :]).astype(BF16)
-            return carry
-
-        lax.fori_loop(0, NX, give, 0)
+        terms = delta[here, :]
+        for xx in range(NX):
+            sib_send[k, xx] = nn(terms, wup_t[:, features(xx * 2 + (1 - c))]).astype(BF16)
         remote(sib_send.at[k], sib_recv.at[k], sib_ss.at[k], sib_rs.at[k], e, sib).start()
         line = jnp.sum(jnp.where(eye, score, 0.0), axis=0, keepdims=True)
         sc_send[k] = line
@@ -221,11 +242,8 @@
 
         lax.fori_loop(1, HEAD, tell, 0)
 
-        def keep(xx, carry):
-            own[k, xx] = nt(delta[here, :], wup[features(xx * 2 + c), :])
-            return carry
-
-        lax.fori_loop(0, NX, keep, 0)
+        for xx in range(NX):
+            own[k, xx] = nn(terms, wup_t[:, features(xx * 2 + c)])
 
     def pair(k, xx, start, size):
         at = lax.rem(xx + NX, NX)
@@ -257,77 +275,42 @@
         total = sc_recv[k, 0]
         for i in range(1, HEAD):
             total = total + sc_recv[k, i]
-        column = jnp.sum(jnp.where(eye, total, 0.0), axis=1, keepdims=True)
-        ret_send[here, FL:RET] = jnp.broadcast_to(column, (CH, 128)).astype(BF16)
+        total = jnp.sum(jnp.where(eye, total, 0.0), axis=1, keepdims=True)
+        ret_send[here, FL:RET] = jnp.broadcast_to(total, (CH, 128)).astype(BF16)
         wait_recv(m2r.at[k, 0], m2_rs.at[k, 0])
         wait_recv(m2r.at[k, 1], m2_rs.at[k, 1])
         done = pair(k, x, 0, FL) + m2r[k, 0].astype(F32) + m2r[k, 1].astype(F32)
         ret_send[here, 0:FL] = done.astype(BF16)
 
-        def one(j, carry):
-            p = k * NZ + j
+        for p in range(max(k * PER, 1), (k + 1) * PER):
+            dz, dy = ORDER[p]
             remote(
                 ret_send.at[block(p)], ret_recv.at[block(p)], r_ss.at[0], r_rs.at[k],
-                exp_of(z + j, y + k), h,
+                exp_of(z + dz, y + dy), h,
             ).start()
-            return carry
-
-        lax.fori_loop(1 if k == 0 else 0, NZ, one, 0)
         if k == 0:
             ret_recv[0:CAP, :] = ret_send[0:CAP, :]
 
     def weights_down():
-        def step(hh, carry):
-            gdn[:, features(hh)] = tn(scaled[...], rows[hh, :, FL:XD]).astype(BF16)
-            return carry
-
-        lax.fori_loop(0, HEAD, step, 0)
-        pltpu.make_async_copy(gdn, gdn_out.at[0], o_sem.at[1]).start()
+        flat = scaled[...].T
+        for hh in range(HEAD):
+            gdn[0, :, hh * FL:(hh + 1) * FL] = nn(flat, rows[hh, :, FL:XD]).astype(BF16)
 
     def weights_up():
-        def step(hh, carry):
-            gup[features(hh), :] = tn(rows[hh, :, 0:FL], delta[...]).astype(BF16)
-            return carry
-
-        lax.fori_loop(0, HEAD, step, 0)
-        pltpu.make_async_copy(gup, gup_out.at[0], o_sem.at[0]).start()
-
-    gather1(0)
-    gather1(1)
-    gather2(0)
-    gather1(2)
-    gather2(1)
-    gather3(0)
-    gather1(3)
-    gather2(2)
-    gather3(1)
-    gather4(0)
-    load_up.wait()
-    load_dn.wait()
-    compute(0)
-    gather2(3)
-    gather3(2)
-    reduce1(0)
-    gather4(1)
-    compute(1)
-    reduce2(0)
-    gather3(3)
-    reduce1(1)
-    gather4(2)
-    compute(2)
-    reduce3(0)
-    reduce2(1)
-    reduce1(2)
-    gather4(3)
-    compute(3)
-    reduce3(1)
-    reduce2(2)
-    reduce1(3)
-    weights_down()
-    reduce3(2)
-    reduce2(3)
-    weights_up()
-    reduce3(3)
+        for hh in range(HEAD):
+            gup[0, hh * FL:(hh + 1) * FL, :] = tn(rows[hh, :, 0:FL], delta[...]).astype(BF16)
+
+    stages = (gather1, gather2, gather3, gather4, compute, reduce1, reduce2, reduce3)
+    lags = (0, 1, 2, 3, 3, 4, 5, 6)
+    for tick in range(NCH + lags[-1]):
+        for stage, lag in zip(stages, lags):
+            k = tick - lag
+            if 0 <= k < NCH:
+                stage(k)
+                if k == NCH - 1 and stage is compute:
+                    weights_down()
+                if k == NCH - 1 and stage is reduce1:
+                    weights_up()
 
     back0 = jnp.zeros((TOK, RET), F32)
     back1 = jnp.zeros((TOK, RET), F32)
@@ -339,8 +322,9 @@
         back0 = back0 + nn(pt0[:, rows_of(k)], ret_recv[rows_of(k), :])
         back1 = back1 + nn(pt1[:, rows_of(k)], ret_recv[rows_of(k), :])
     gt_out[...] = (back0[:, 0:FL] + back1[:, 0:FL]).astype(BF16)
-    gg_out[:, 0:1] = back0[:, FL:FL + 1].astype(BF16)
-    gg_out[:, 1:2] = back1[:, FL:FL + 1].astype(BF16)
+    for i, back in enumerate((back0, back1)):
+        line = jnp.sum(jnp.where(lane == sub, back[:, FL:RET], 0.0), axis=0, keepdims=True)
+        gg_out[i:i + 1, :] = line.astype(BF16)
 
     wait_send(send.at[pl.ds(CAP, ROWS - CAP)], d_send.at[0])
     whole = rows.at[0, :, pl.ds(0, XD)]
@@ -358,29 +342,32 @@
             wait_send(m2s.at[k, i], m2_ss.at[k, i])
         wait_send(sc_recv.at[k, pl.ds(0, HEAD - 1)], sc_ss.at[k])
     wait_send(ret_send.at[pl.ds(CAP, ROWS - CAP)], r_ss.at[0])
-    pltpu.make_async_copy(gdn, gdn_out.at[0], o_sem.at[1]).wait()
-    pltpu.make_async_copy(gup, gup_out.at[0], o_sem.at[0]).wait()
+
+
+def store(*refs):
+    ins, outs, sem = refs[:4], refs[4:8], refs[8]
+    copies = [pltpu.make_async_copy(ins[i], outs[i], sem.at[i]) for i in range(4)]
+    for one in copies:
+        one.start()
+    for one in copies:
+        one.wait()
 
 
 def shards(tokens, cotangent, gates, expert_ids, w_up, w_down):
     vmem = pl.BlockSpec(memory_space=pltpu.VMEM)
     hbm = pl.BlockSpec(memory_space=pl.ANY)
     dma = pltpu.SemaphoreType.DMA
-    return pl.pallas_call(
+    shapes = ((TOK, FL), (2, TOK), (1, D, HID), (1, HID, D))
+    results = pl.pallas_call(
         kernel,
-        out_shape=(
-            jax.ShapeDtypeStruct((TOK, FL), BF16),
-            jax.ShapeDtypeStruct((TOK, 2), BF16),
-            jax.ShapeDtypeStruct((1, D, HID), BF16),
-            jax.ShapeDtypeStruct((1, HID, D), BF16),
-        ),
+        out_shape=tuple(pltpu.VMEM(shape, BF16) for shape in shapes),
         in_specs=[vmem, vmem, vmem, vmem, hbm, hbm],
-        out_specs=(vmem, vmem, hbm, hbm),
+        out_specs=(vmem, vmem, vmem, vmem),
         scratch_shapes=[
             pltpu.VMEM((D, HID), BF16),
             pltpu.VMEM((HID, D), BF16),
+            pltpu.VMEM((HID, D), BF16),
             pltpu.VMEM((D, HID), BF16),
-            pltpu.VMEM((HID, D), BF16),
             pltpu.VMEM((TOK, ROWS), BF16),
             pltpu.VMEM((TOK, ROWS), BF16),
             pltpu.VMEM((ROWS, MSG), BF16),
@@ -394,11 +381,10 @@
             pltpu.VMEM((NCH, 2, CH, FL // 2), BF16),
             pltpu.VMEM((NCH, 2, CH, FL), BF16),
             pltpu.VMEM((NCH, 2, CH, FL), BF16),
-            pltpu.VMEM((NCH, 1, CH), F32),
-            pltpu.VMEM((NCH, HEAD, 1, CH), F32),
+            pltpu.VMEM((NCH, 1, 128), F32),
+            pltpu.VMEM((NCH, HEAD, 1, 128), F32),
             pltpu.VMEM((ROWS, RET), BF16),
             pltpu.VMEM((ROWS, RET), BF16),
-            dma((2,)),
             dma((2,)),
             dma((1,)), dma((NCH,)),
             dma((1,)), dma((NCH,)),
@@ -418,7 +404,16 @@
         cost_estimate=pl.CostEstimate(
             flops=10 * ROWS * D * HID, bytes_accessed=8 * D * HID, transcendentals=2 * ROWS * HID
         ),
-    )(tokens, cotangent, gates, expert_ids, w_up, w_down)
+    )(tokens, cotangent, gates.T, expert_ids.T, w_up, w_down)
+    grad_tokens, grad_gates, grad_up, grad_down = pl.pallas_call(
+        store,
+        out_shape=tuple(jax.ShapeDtypeStruct(shape, BF16) for shape in shapes),
+        in_specs=[vmem] * 4,
+        out_specs=(hbm,) * 4,
+        scratch_shapes=[dma((4,))],
+        compiler_params=pltpu.CompilerParams(vmem_limit_bytes=16 * 1024 * 1024),
+    )(*results)
+    return grad_tokens, grad_gates.T, grad_up, grad_down
 
 
 def solution(mesh):

time: 102 us -> 88.9 us (0.87)
  local copies, waits for them, and re-layouts: 10.2 us -> 0 us
  Pallas kernels: 90.9 us -> 88 us
    unnamed x7 -> x0, local copies, waits for them, and re-layouts: 8.88 us -> none
    pallas_call x1 -> x2, Pallas kernels: 90.9 us -> 88 us  [the longest x1 85.9 us: shards(): pl.pallas_call(kernel, out_shape=tuple((pltpu.VMEM(shape, BF16) for shape...]
    pallas_call x1 -> x0, local copies, waits for them, and re-layouts: 1.35 us -> none  [shards(): pl.pallas_call(kernel, out_shape=(jax.ShapeDtypeStruct((TOK, FL), BF16),...]
where the time goes in v2:
time: 88.9 us; the launch traced here: 88.8 us
  Pallas kernels  88 us (99%)
    pallas_call x1, Pallas kernels, shards(): pl.pallas_call(kernel, out_shape=tuple((pltpu.VMEM(shape, BF16) for shape...  85.9 us
    pallas_call x1, Pallas kernels, shards(): pl.pallas_call(store, out_shape=tuple((jax.ShapeDtypeStruct(shape, BF16)...  2.09 us

profile of v2, /device:TPU:2, one launch (start us, length us, event | category | flops | bytes accessed | tf_op | source)
XLA Modules:
  0.0 88.8 jit_solution(2726839978531031424)
XLA Ops:
  0.6 85.9 %shard_map.93 = (bf16[128,512]{1,0:T(8,128)(2,1)S(1)}, bf16[2,128]{1,0:T(2,128)(2,1)S(1)}, bf16[1,4096,256]{2,1,0:T(8,128)(2,1)S(1)}, bf16[1,256,4096]{2,1,0:T(8,128)(2,1)S(1)}) custom-call(bf16[128,512]{1,0:T(8,128)(2,1)} %tok_ref.1, bf16[128,512]{1,0:T(8,128)(2,1)} %cot_ref.1, bf16[2,128]{1,0:T(2,128)(2,1)} %bitcast.4, s32[2,128]{1,0:T(2,128)} %bitcast.3, ...), custom_call_target="tpu_custom_call" | custom-call | flops 5368709120 | bytes 8388608 | tf_op jit(solution)/shard_map/pallas_call | solution.py:361
  86.5 2.1 %shard_map.94 = (bf16[128,512]{1,0:T(8,128)(2,1)}, bf16[2,128]{1,0:T(2,128)(2,1)}, bf16[1,4096,256]{2,1,0:T(8,128)(2,1)}, bf16[1,256,4096]{2,1,0:T(8,128)(2,1)}) custom-call(bf16[128,512]{1,0:T(8,128)(2,1)S(1)} %get-tuple-element.12.refs_0_, bf16[2,128]{1,0:T(2,128)(2,1)S(1)} %get-tuple-element.13.refs_1_, ...), custom_call_target="tpu_custom_call" | custom-call | tf_op jit(solution)/shard_map/pallas_call | solution.py:408

commit v3 on v2

--- a/solution.py
+++ b/solution.py
@@ -22,13 +22,12 @@
 HID = 256
 D = HEAD * FL
 XD = 2 * FL
-MSG = XD + 128
-RET = FL + 128
+LINE = 128
 
 
 def offsets():
     order = []
-    for reach, late in ((0, 0), (1, 0), (2, 0), (3, 0), (4, 0), (3, 1), (2, 1), (1, 1)):
+    for reach, late in ((0, 0), (2, 0), (3, 0), (4, 0), (1, 0), (3, 1), (2, 1), (1, 1)):
         if reach in (0, NZ // 2):
             order += [(reach, 0), (reach, 1), (reach, NY - 1), (reach, 2)]
         elif late:
@@ -39,6 +38,19 @@
 
 
 ORDER = offsets()
+NEAR = (0, 4, 7)
+FAR = (1, 6, 3, 2, 5)
+AHEAD = 3
+PLAN = (
+    ("g1", 1), ("d", 2), ("pass", 0), ("g1", 6), ("d", 5), ("g2", 1), ("near", 0), ("g2", 6),
+    ("g1", 3), ("g3", 1), ("g3", 6), ("c", 1), ("g1", 2), ("g2", 3), ("near", 4), ("g3", 0),
+    ("c", 6), ("r1", 1), ("g2", 2), ("g1", 5), ("near", 7), ("g3", 3), ("c", 0), ("r1", 6),
+    ("r2", 1), ("g3", 2), ("c", 3), ("r1", 0), ("g2", 5), ("r2", 6), ("g3", 4), ("r3", 1),
+    ("c", 2), ("r1", 3), ("r2", 0), ("g3", 5), ("r3", 6), ("c", 4), ("r1", 2), ("r2", 3),
+    ("g3", 7), ("r3", 0), ("c", 5), ("r1", 4), ("r2", 2), ("r3", 3), ("c", 7), ("r1", 5),
+    ("r2", 4), ("r3", 2), ("wd", 0), ("r1", 7), ("r2", 5), ("wu", 0), ("r3", 4), ("r2", 7),
+    ("r3", 5), ("r3", 7),
+)
 
 
 def gelu_parts(pre):
@@ -63,10 +75,10 @@
 def kernel(
     tok_ref, cot_ref, gates_ref, ids_ref, wup_hbm, wdn_hbm,
     gt_out, gg_out, gup, gdn,
-    wup, wdn, wup_t, wdn_t, pt0, pt1, send, rows, scaled, delta,
+    wup, wdn, wup_t, wdn_t, pt0, pt1, raw, send, near, rows, gate_lines, gate_in, score_lines, score_in, scaled, delta,
     sib_send, sib_recv, own, m1s, m1r, m2s, m2r, sc_send, sc_recv, ret_send, ret_recv,
     w_sem,
-    d_send, d_recv, ga_send, ga_recv, gb_send, gb_recv, a2_send, a2_recv, b2_send, b2_recv,
+    t_send, t_recv, n_send, n_recv, d_send, d_recv, gl_send, gl_recv, sl_send, sl_recv, ga_send, ga_recv, gb_send, gb_recv, a2_send, a2_recv, b2_send, b2_recv,
     gs_send, gs_recv, sib_ss, sib_rs, m1_ss, m1_rs, m2_ss, m2_rs, sc_ss, sc_rs, r_ss, r_rs,
 ):
     e, h = lax.axis_index("exp"), lax.axis_index("head")
@@ -76,7 +88,8 @@
     def head_of(xx, cc):
         return lax.rem(xx + NX, NX) * 2 + cc
 
-    right, left, opp = head_of(x + 1, c), head_of(x - 1, c), head_of(x + 2, c)
+    xr, xl, xo = lax.rem(x + 1, NX), lax.rem(x + NX - 1, NX), lax.rem(x + 2, NX)
+    right, left = head_of(x + 1, c), head_of(x - 1, c)
     sib = x * 2 + (1 - c)
 
     def exp_of(zz, yy):
@@ -122,8 +135,18 @@
     slots = lax.broadcasted_iota(I32, (TOK, ROWS), 1)
     pt0[...] = (d0 == slots).astype(BF16)
     pt1[...] = (d1 == slots).astype(BF16)
-    gate0 = jnp.broadcast_to(column(gates_ref, 0), (TOK, 128)).astype(BF16)
-    gate1 = jnp.broadcast_to(column(gates_ref, 1), (TOK, 128)).astype(BF16)
+    gates = [jnp.broadcast_to(gates_ref[k:k + 1, :], (16, TOK)) for k in range(2)]
+    gate_row = (nn(gates[0], pt0[...]) + nn(gates[1], pt1[...]))[0:1, :]
+    for i in range(ROWS // LINE):
+        gate_lines[i] = gate_row[:, i * LINE:(i + 1) * LINE]
+    gate_in[0] = gate_lines[0]
+    slot_of = lax.broadcasted_iota(I32, (1, LINE), 1) // CAP
+
+    def merge(ref, first, count):
+        line = jnp.zeros((1, LINE), F32)
+        for p in range(first, first + count):
+            line = jnp.where(slot_of == p % 8, ref[p], line)
+        return line
 
     def rows_of(k):
         return pl.ds(k * CH, CH)
@@ -134,10 +157,13 @@
     def fill(k):
         here = rows_of(k)
         p0, p1 = pt0[:, here], pt1[:, here]
-        both = p0 + p1
-        send[here, 0:FL] = tn(both, tok_ref[...]).astype(BF16)
-        send[here, FL:XD] = tn(both, cot_ref[...]).astype(BF16)
-        send[here, XD:MSG] = (tn(p0, gate0) + tn(p1, gate1)).astype(BF16)
+        send[here, :] = tn(p0 + p1, raw[x]).astype(BF16)
+
+    def fill_near(k):
+        here, there = rows_of(k), rows_of(NEAR.index(k))
+        p0, p1 = pt0[:, here], pt1[:, here]
+        for xx in range(NX):
+            near[xx, there, :] = tn(p0 + p1, raw[xx]).astype(BF16)
 
     def remote(src, dst, ss, rs, exp_i, head_i):
         return pltpu.make_async_remote_copy(
@@ -145,27 +171,50 @@
             device_id=(exp_i, head_i), device_id_type=MESH,
         )
 
-    def dispatch(k):
+    def send_gates(k):
         for p in range(max(k * PER, 1), (k + 1) * PER):
             dz, dy = ORDER[p]
             remote(
-                send.at[block(p)], rows.at[h, block(p)], d_send.at[0], d_recv.at[k],
+                gate_lines.at[p // 8], gate_in.at[p], gl_send.at[0], gl_recv.at[k], exp_of(z - dz, y - dy), h
+            ).start()
+
+    def dispatch(k):
+        for p in range(k * PER, (k + 1) * PER):
+            dz, dy = ORDER[p]
+            remote(
+                send.at[block(p)], rows.at[c, x, block(p)], d_send.at[0], d_recv.at[k],
                 exp_of(z - dz, y - dy), h,
             ).start()
 
+    def dispatch_near(k):
+        for p in range(max(k * PER, 1), (k + 1) * PER):
+            dz, dy = ORDER[p]
+            remote(
+                near.at[:, block(p + (NEAR.index(k) - k) * PER)], rows.at[c, :, block(p)],
+                n_send.at[0], n_recv.at[k], exp_of(z - dz, y - dy), h,
+            ).start()
+
     def wait_recv(ref, rs):
         remote(ref, ref, rs, rs, e, sib).wait_recv()
 
     def wait_send(ref, ss):
         remote(ref, ref, ss, ss, e, sib).wait_send()
 
-    fill(0)
+    raw[x, :, 0:FL] = tok_ref[...]
+    raw[x, :, FL:XD] = cot_ref[...]
+    fill(FAR[0])
     pl.semaphore_wait(barrier, EXP - 1 + HEAD - 1)
-    dispatch(0)
-    rows[h, 0:CAP, :] = send[0:CAP, :]
-    for k in range(1, NCH):
+    mine = raw.at[x]
+    remote(mine, mine, t_send.at[0], t_recv.at[0], e, right).start()
+    remote(mine, mine, t_send.at[1], t_recv.at[1], e, left).start()
+    dispatch(FAR[0])
+    for k in FAR[1:AHEAD]:
         fill(k)
         dispatch(k)
+    for k in FAR[AHEAD:]:
+        fill(k)
+    for k in range(NCH):
+        send_gates(k)
     load_up.wait()
     load_dn.wait()
     for hh in range(HEAD):
@@ -173,54 +222,84 @@
         wup_t[:, part_of] = wup[part_of, :].T
         wdn_t[part_of, :] = wdn[:, part_of].T
 
-    def part(hh, k, start=0, size=CH):
-        return rows.at[hh, pl.ds(k * CH + start, size), pl.ds(0, XD)]
+    def pass_raw(k):
+        low, high = raw.at[xl, pl.ds(0, TOK // 2)], raw.at[xr, pl.ds(TOK // 2, TOK // 2)]
+        wait_recv(raw.at[xl], t_recv.at[0])
+        remote(low, low, t_send.at[2], t_recv.at[2], e, right).start()
+        wait_recv(raw.at[xr], t_recv.at[1])
+        remote(high, high, t_send.at[3], t_recv.at[3], e, left).start()
+
+    def send_near(k):
+        if k == NEAR[0]:
+            wait_recv(raw.at[xo, pl.ds(0, TOK // 2)], t_recv.at[2])
+            wait_recv(raw.at[xo, pl.ds(TOK // 2, TOK // 2)], t_recv.at[3])
+        fill_near(k)
+        dispatch_near(k)
+        if k == 0:
+            rows[c, :, 0:CAP, :] = near[:, 0:CAP, :]
+
+    def part(xx, k, start=0, size=CH):
+        return rows.at[c, xx, pl.ds(k * CH + start, size)]
+
+    def whole(cc, k, start=0):
+        return rows.at[cc, :, pl.ds(k * CH + start, CH - start)]
 
     half = CH // 2
 
     def gather1(k):
-        if k == 0:
-            wait_recv(rows.at[h, pl.ds(CAP, CH - CAP)], d_recv.at[k])
+        if k in FAR:
+            wait_recv(rows.at[c, x, rows_of(k)], d_recv.at[k])
+            mine = part(x, k)
+            remote(mine, mine, ga_send.at[0], ga_recv.at[k], e, right).start()
+            remote(mine, mine, gb_send.at[0], gb_recv.at[k], e, left).start()
+            remote(mine, mine, gs_send.at[0], gs_recv.at[k, 0], e, sib).start()
+
+    def gather2(k):
+        if k in FAR:
+            low, high = part(xl, k, 0, half), part(xr, k, half, half)
+            wait_recv(part(xl, k), ga_recv.at[k])
+            remote(low, low, a2_send.at[0], a2_recv.at[k], e, right).start()
+            remote(part(xl, k), part(xl, k), gs_send.at[1], gs_recv.at[k, 1], e, sib).start()
+            wait_recv(part(xr, k), gb_recv.at[k])
+            remote(high, high, b2_send.at[0], b2_recv.at[k], e, left).start()
+            remote(part(xr, k), part(xr, k), gs_send.at[2], gs_recv.at[k, 2], e, sib).start()
+
+    def gather3(k):
+        if k in FAR:
+            wait_recv(part(xo, k, 0, half), a2_recv.at[k])
+            wait_recv(part(xo, k, half, half), b2_recv.at[k])
+            remote(part(xo, k), part(xo, k), gs_send.at[3], gs_recv.at[k, 3], e, sib).start()
         else:
-            wait_recv(rows.at[h, rows_of(k)], d_recv.at[k])
-        mine = part(h, k)
-        remote(mine, mine, ga_send.at[0], ga_recv.at[k], e, right).start()
-        remote(mine, mine, gb_send.at[0], gb_recv.at[k], e, left).start()
-        remote(mine, mine, gs_send.at[0], gs_recv.at[k, 0], e, sib).start()
-
-    def gather2(k):
-        low, high = part(left, k, 0, half), part(right, k, half, half)
-        wait_recv(part(left, k), ga_recv.at[k])
-        remote(low, low, a2_send.at[0], a2_recv.at[k], e, right).start()
-        remote(part(left, k), part(left, k), gs_send.at[1], gs_recv.at[k, 1], e, sib).start()
-        wait_recv(part(right, k), gb_recv.at[k])
-        remote(high, high, b2_send.at[0], b2_recv.at[k], e, left).start()
-        remote(part(right, k), part(right, k), gs_send.at[2], gs_recv.at[k, 2], e, sib).start()
-
-    def gather3(k):
-        wait_recv(part(opp, k, 0, half), a2_recv.at[k])
-        wait_recv(part(opp, k, half, half), b2_recv.at[k])
-        remote(part(opp, k), part(opp, k), gs_send.at[3], gs_recv.at[k, 3], e, sib).start()
+            start = CAP if k == 0 else 0
+            wait_recv(whole(c, k, start), n_recv.at[k])
+            remote(whole(c, k), whole(c, k), gs_send.at[4], gs_recv.at[k, 0], e, sib).start()
 
     def gather4(k):
-        for i in range(4):
-            wait_recv(part(h, k), gs_recv.at[k, i])
-
-    eye = lane[0:CH] == sub[0:CH]
+        if k in FAR:
+            for i in range(4):
+                wait_recv(part(x, k), gs_recv.at[k, i])
+        else:
+            wait_recv(whole(1 - c, k), gs_recv.at[k, 0])
+
+    def eye(k):
+        return lane[0:CH] == sub[0:CH] + k % 2 * CH
 
     def features(hh):
         return pl.ds(pl.multiple_of(hh * FL, FL), FL)
 
     def compute(k):
+        gather4(k)
         here = rows_of(k)
 
         pre = jnp.zeros((CH, HID), F32)
         back = jnp.zeros((CH, HID), F32)
         for hh in range(HEAD):
             part_of = pl.ds(hh * FL, FL)
-            pre = pre + nn(rows[hh, here, 0:FL], wup[part_of, :])
-            back = back + nn(rows[hh, here, FL:XD], wdn_t[part_of, :])
-        g = rows[h, here, XD:MSG][:, 0:1].astype(F32)
+            pre = pre + nn(rows[hh % 2, hh // 2, here, 0:FL], wup[part_of, :])
+            back = back + nn(rows[hh % 2, hh // 2, here, FL:XD], wdn_t[part_of, :])
+        first = 1 if k == 0 else 0
+        wait_recv(gate_in.at[pl.ds(k * PER + first, PER - first)], gl_recv.at[k])
+        g = jnp.sum(jnp.where(eye(k), merge(gate_in, k * PER, PER), 0.0), axis=1, keepdims=True)
         act, slope = gelu_parts(pre)
         score = jnp.sum(back * act, axis=1, keepdims=True)
         scaled[here, :] = (g * act).astype(BF16)
@@ -230,7 +309,7 @@
         for xx in range(NX):
             sib_send[k, xx] = nn(terms, wup_t[:, features(xx * 2 + (1 - c))]).astype(BF16)
         remote(sib_send.at[k], sib_recv.at[k], sib_ss.at[k], sib_rs.at[k], e, sib).start()
-        line = jnp.sum(jnp.where(eye, score, 0.0), axis=0, keepdims=True)
+        line = jnp.sum(jnp.where(eye(k), score, 0.0), axis=0, keepdims=True)
         sc_send[k] = line
         sc_recv[k, h] = line
 
@@ -275,64 +354,74 @@
         total = sc_recv[k, 0]
         for i in range(1, HEAD):
             total = total + sc_recv[k, i]
-        total = jnp.sum(jnp.where(eye, total, 0.0), axis=1, keepdims=True)
-        ret_send[here, FL:RET] = jnp.broadcast_to(total, (CH, 128)).astype(BF16)
+        score_lines[k] = total.astype(BF16).astype(F32)
         wait_recv(m2r.at[k, 0], m2_rs.at[k, 0])
         wait_recv(m2r.at[k, 1], m2_rs.at[k, 1])
         done = pair(k, x, 0, FL) + m2r[k, 0].astype(F32) + m2r[k, 1].astype(F32)
-        ret_send[here, 0:FL] = done.astype(BF16)
+        ret_send[here, :] = done.astype(BF16)
 
         for p in range(max(k * PER, 1), (k + 1) * PER):
             dz, dy = ORDER[p]
+            to = exp_of(z + dz, y + dy)
             remote(
-                ret_send.at[block(p)], ret_recv.at[block(p)], r_ss.at[0], r_rs.at[k],
-                exp_of(z + dz, y + dy), h,
+                ret_send.at[block(p)], ret_recv.at[block(p)], r_ss.at[0], r_rs.at[k], to, h
+            ).start()
+            remote(
+                score_lines.at[k], score_in.at[p], sl_send.at[0], sl_recv.at[0], to, h
             ).start()
         if k == 0:
             ret_recv[0:CAP, :] = ret_send[0:CAP, :]
-
-    def weights_down():
+            score_in[0] = score_lines[0]
+
+    def weights_down(k):
         flat = scaled[...].T
         for hh in range(HEAD):
-            gdn[0, :, hh * FL:(hh + 1) * FL] = nn(flat, rows[hh, :, FL:XD]).astype(BF16)
-
-    def weights_up():
+            gdn[0, :, hh * FL:(hh + 1) * FL] = nn(flat, rows[hh % 2, hh // 2, :, FL:XD]).astype(BF16)
+
+    def weights_up(k):
         for hh in range(HEAD):
-            gup[0, hh * FL:(hh + 1) * FL, :] = tn(rows[hh, :, 0:FL], delta[...]).astype(BF16)
-
-    stages = (gather1, gather2, gather3, gather4, compute, reduce1, reduce2, reduce3)
-    lags = (0, 1, 2, 3, 3, 4, 5, 6)
-    for tick in range(NCH + lags[-1]):
-        for stage, lag in zip(stages, lags):
-            k = tick - lag
-            if 0 <= k < NCH:
-                stage(k)
-                if k == NCH - 1 and stage is compute:
-                    weights_down()
-                if k == NCH - 1 and stage is reduce1:
-                    weights_up()
-
-    back0 = jnp.zeros((TOK, RET), F32)
-    back1 = jnp.zeros((TOK, RET), F32)
+            gup[0, hh * FL:(hh + 1) * FL, :] = tn(rows[hh % 2, hh // 2, :, 0:FL], delta[...]).astype(BF16)
+
+    stages = {
+        "pass": pass_raw, "d": dispatch, "near": send_near, "g1": gather1, "g2": gather2, "g3": gather3,
+        "c": compute, "r1": reduce1, "r2": reduce2, "r3": reduce3, "wd": weights_down, "wu": weights_up,
+    }
+    for stage, k in PLAN:
+        stages[stage](k)
+
+    total = jnp.zeros((TOK, FL), F32)
     for k in range(NCH):
+        here = rows_of(k)
         if k == 0:
             wait_recv(ret_recv.at[pl.ds(CAP, CH - CAP)], r_rs.at[k])
         else:
-            wait_recv(ret_recv.at[rows_of(k)], r_rs.at[k])
-        back0 = back0 + nn(pt0[:, rows_of(k)], ret_recv[rows_of(k), :])
-        back1 = back1 + nn(pt1[:, rows_of(k)], ret_recv[rows_of(k), :])
-    gt_out[...] = (back0[:, 0:FL] + back1[:, 0:FL]).astype(BF16)
-    for i, back in enumerate((back0, back1)):
-        line = jnp.sum(jnp.where(lane == sub, back[:, FL:RET], 0.0), axis=0, keepdims=True)
-        gg_out[i:i + 1, :] = line.astype(BF16)
-
-    wait_send(send.at[pl.ds(CAP, ROWS - CAP)], d_send.at[0])
-    whole = rows.at[0, :, pl.ds(0, XD)]
-    wait_send(whole, ga_send.at[0])
-    wait_send(whole, gb_send.at[0])
+            wait_recv(ret_recv.at[here], r_rs.at[k])
+        total = total + nn(pt0[:, here] + pt1[:, here], ret_recv[here, :])
+    gt_out[...] = total.astype(BF16)
+    wait_recv(score_in.at[pl.ds(1, EXP - 1)], sl_recv.at[0])
+    for k, pt in enumerate((pt0, pt1)):
+        picked = jnp.zeros((TOK, LINE), F32)
+        for i in range(ROWS // LINE):
+            picked = picked + pt[:, i * LINE:(i + 1) * LINE].astype(F32) * merge(score_in, i * 8, 8)
+        score = jnp.sum(picked, axis=1, keepdims=True)
+        gg_out[k:k + 1, :] = jnp.sum(jnp.where(lane == sub, score, 0.0), axis=0, keepdims=True).astype(BF16)
+
+    wait_send(raw.at[0], t_send.at[0])
+    wait_send(raw.at[0], t_send.at[1])
+    wait_send(raw.at[0, pl.ds(0, TOK // 2)], t_send.at[2])
+    wait_send(raw.at[0, pl.ds(0, TOK // 2)], t_send.at[3])
+    far_rows, near_rows = len(FAR) * CH, len(NEAR) * CH
+    wait_send(send.at[pl.ds(0, far_rows)], d_send.at[0])
+    wait_send(near.at[:, pl.ds(CAP, near_rows - CAP)], n_send.at[0])
+    wait_send(gate_in.at[pl.ds(1, EXP - 1)], gl_send.at[0])
+    wait_send(score_in.at[pl.ds(1, EXP - 1)], sl_send.at[0])
+    gathered = rows.at[0, 0, pl.ds(0, far_rows)]
+    wait_send(gathered, ga_send.at[0])
+    wait_send(gathered, gb_send.at[0])
     for i in range(4):
-        wait_send(whole, gs_send.at[i])
-    halves = rows.at[0, pl.ds(0, ROWS // 2), pl.ds(0, XD)]
+        wait_send(gathered, gs_send.at[i])
+    wait_send(rows.at[0, :, pl.ds(0, near_rows)], gs_send.at[4])
+    halves = rows.at[0, 0, pl.ds(0, far_rows // 2)]
     wait_send(halves, a2_send.at[0])
     wait_send(halves, b2_send.at[0])
     for k in range(NCH):
@@ -370,8 +459,14 @@
             pltpu.VMEM((D, HID), BF16),
             pltpu.VMEM((TOK, ROWS), BF16),
             pltpu.VMEM((TOK, ROWS), BF16),
-            pltpu.VMEM((ROWS, MSG), BF16),
-            pltpu.VMEM((HEAD, ROWS, MSG), BF16),
+            pltpu.VMEM((NX, TOK, XD), BF16),
+            pltpu.VMEM((ROWS, XD), BF16),
+            pltpu.VMEM((NX, len(NEAR) * CH, XD), BF16),
+            pltpu.VMEM((2, NX, ROWS, XD), BF16),
+            pltpu.VMEM((ROWS // LINE, 1, LINE), F32),
+            pltpu.VMEM((EXP, 1, LINE), F32),
+            pltpu.VMEM((NCH, 1, LINE), F32),
+            pltpu.VMEM((EXP, 1, LINE), F32),
             pltpu.VMEM((ROWS, HID), BF16),
             pltpu.VMEM((ROWS, HID), BF16),
             pltpu.VMEM((NCH, NX, CH, FL), BF16),
@@ -381,17 +476,21 @@
             pltpu.VMEM((NCH, 2, CH, FL // 2), BF16),
             pltpu.VMEM((NCH, 2, CH, FL), BF16),
             pltpu.VMEM((NCH, 2, CH, FL), BF16),
-            pltpu.VMEM((NCH, 1, 128), F32),
-            pltpu.VMEM((NCH, HEAD, 1, 128), F32),
-            pltpu.VMEM((ROWS, RET), BF16),
-            pltpu.VMEM((ROWS, RET), BF16),
+            pltpu.VMEM((NCH, 1, LINE), F32),
+            pltpu.VMEM((NCH, HEAD, 1, LINE), F32),
+            pltpu.VMEM((ROWS, FL), BF16),
+            pltpu.VMEM((ROWS, FL), BF16),
             dma((2,)),
-            dma((1,)), dma((NCH,)),
-            dma((1,)), dma((NCH,)),
-            dma((1,)), dma((NCH,)),
-            dma((1,)), dma((NCH,)),
-            dma((1,)), dma((NCH,)),
-            dma((4,)), dma((NCH, 4)),
+            dma((4,)), dma((4,)),
+            dma((1,)), dma((NCH,)),
+            dma((1,)), dma((NCH,)),
+            dma((1,)), dma((NCH,)),
+            dma((1,)), dma((1,)),
+            dma((1,)), dma((NCH,)),
+            dma((1,)), dma((NCH,)),
+            dma((1,)), dma((NCH,)),
+            dma((1,)), dma((NCH,)),
+            dma((5,)), dma((NCH, 4)),
             dma((NCH,)), dma((NCH,)),
             dma((NCH, 2)), dma((NCH, 2)),
             dma((NCH, 2)), dma((NCH, 2)),

time: 88.9 us -> 83 us (0.934)
  Pallas kernels: 88 us -> 81.5 us
    pallas_call x1, Pallas kernels: 85.9 us -> 79.4 us  [shards(): pl.pallas_call(kernel, out_shape=tuple((pltpu.VMEM(shape, BF16) for shape...]
where the time goes in v3:
time: 83 us; the launch traced here: 82.3 us
  Pallas kernels  81.5 us (98%)
    pallas_call x1, Pallas kernels, shards(): pl.pallas_call(kernel, out_shape=tuple((pltpu.VMEM(shape, BF16) for shape...  79.4 us
    pallas_call x1, Pallas kernels, shards(): pl.pallas_call(store, out_shape=tuple((jax.ShapeDtypeStruct(shape, BF16)...  2.09 us

profile of v3, /device:TPU:2, one launch (start us, length us, event | category | flops | bytes accessed | tf_op | source)
XLA Modules:
  0.0 82.3 jit_solution(885075966288022459)
XLA Ops:
  0.6 79.4 %shard_map.93 = (bf16[128,512]{1,0:T(8,128)(2,1)S(1)}, bf16[2,128]{1,0:T(2,128)(2,1)S(1)}, bf16[1,4096,256]{2,1,0:T(8,128)(2,1)S(1)}, bf16[1,256,4096]{2,1,0:T(8,128)(2,1)S(1)}) custom-call(bf16[128,512]{1,0:T(8,128)(2,1)} %tok_ref.1, bf16[128,512]{1,0:T(8,128)(2,1)} %cot_ref.1, bf16[2,128]{1,0:T(2,128)(2,1)} %bitcast.4, s32[2,128]{1,0:T(2,128)} %bitcast.3, ...), custom_call_target="tpu_custom_call" | custom-call | flops 5368709120 | bytes 8388608 | tf_op jit(solution)/shard_map/pallas_call | solution.py:450
  80.0 2.1 %shard_map.94 = (bf16[128,512]{1,0:T(8,128)(2,1)}, bf16[2,128]{1,0:T(2,128)(2,1)}, bf16[1,4096,256]{2,1,0:T(8,128)(2,1)}, bf16[1,256,4096]{2,1,0:T(8,128)(2,1)}) custom-call(bf16[128,512]{1,0:T(8,128)(2,1)S(1)} %get-tuple-element.12.refs_0_, bf16[2,128]{1,0:T(2,128)(2,1)S(1)} %get-tuple-element.13.refs_1_, ...), custom_call_target="tpu_custom_call" | custom-call | tf_op jit(solution)/shard_map/pallas_call | solution.py:507

commit v4 on v3

--- a/solution.py
+++ b/solution.py
@@ -27,7 +27,7 @@
 
 def offsets():
     order = []
-    for reach, late in ((0, 0), (2, 0), (3, 0), (4, 0), (1, 0), (3, 1), (2, 1), (1, 1)):
+    for reach, late in ((2, 0), (3, 0), (0, 0), (3, 1), (4, 0), (1, 0), (2, 1), (1, 1)):
         if reach in (0, NZ // 2):
             order += [(reach, 0), (reach, 1), (reach, NY - 1), (reach, 2)]
         elif late:
@@ -38,18 +38,20 @@
 
 
 ORDER = offsets()
-NEAR = (0, 4, 7)
-FAR = (1, 6, 3, 2, 5)
+HOME = 2
+NEAR = (HOME, 5, 7)
+FAR = (0, 1, 3, 4, 6)
 AHEAD = 3
+GROUPS = ((0, 1), (1, 1), (2, 1), (3, 1), (4, 1), (5, 1), (6, 1), (7, 1))
 PLAN = (
-    ("g1", 1), ("d", 2), ("pass", 0), ("g1", 6), ("d", 5), ("g2", 1), ("near", 0), ("g2", 6),
-    ("g1", 3), ("g3", 1), ("g3", 6), ("c", 1), ("g1", 2), ("g2", 3), ("near", 4), ("g3", 0),
-    ("c", 6), ("r1", 1), ("g2", 2), ("g1", 5), ("near", 7), ("g3", 3), ("c", 0), ("r1", 6),
-    ("r2", 1), ("g3", 2), ("c", 3), ("r1", 0), ("g2", 5), ("r2", 6), ("g3", 4), ("r3", 1),
-    ("c", 2), ("r1", 3), ("r2", 0), ("g3", 5), ("r3", 6), ("c", 4), ("r1", 2), ("r2", 3),
-    ("g3", 7), ("r3", 0), ("c", 5), ("r1", 4), ("r2", 2), ("r3", 3), ("c", 7), ("r1", 5),
-    ("r2", 4), ("r3", 2), ("wd", 0), ("r1", 7), ("r2", 5), ("wu", 0), ("r3", 4), ("r2", 7),
-    ("r3", 5), ("r3", 7),
+    ("g1", 0), ("d", 4), ("pass", 0), ("g2", 0), ("g1", 1), ("d", 6), ("near", 2), ("g3", 0),
+    ("g1", 3), ("near", 5), ("g2", 1), ("c", 0), ("g2", 3), ("g3", 1), ("g1", 4), ("near", 7),
+    ("r1", 0), ("g3", 2), ("g3", 3), ("c", 1), ("g1", 6), ("c", 2), ("g2", 4), ("r2", 0),
+    ("r1", 1), ("c", 3), ("g2", 6), ("r1", 2), ("g3", 5), ("g3", 4), ("r1", 3), ("r3", 0),
+    ("r2", 1), ("g3", 6), ("c", 4), ("r2", 2), ("r2", 3), ("g3", 7), ("c", 5), ("r1", 4),
+    ("c", 6), ("c", 7), ("r2", 4), ("r1", 5), ("r3", 1), ("r1", 6), ("r3", 2), ("r3", 3),
+    ("r1", 7), ("r2", 5), ("r2", 6), ("r3", 4), ("r2", 7), ("wd", 0), ("r3", 5), ("r3", 6),
+    ("r3", 7), ("wu", 0),
 )
 
 
@@ -139,7 +141,7 @@
     gate_row = (nn(gates[0], pt0[...]) + nn(gates[1], pt1[...]))[0:1, :]
     for i in range(ROWS // LINE):
         gate_lines[i] = gate_row[:, i * LINE:(i + 1) * LINE]
-    gate_in[0] = gate_lines[0]
+    gate_in[HOME * PER] = gate_lines[HOME * PER // 8]
     slot_of = lax.broadcasted_iota(I32, (1, LINE), 1) // CAP
 
     def merge(ref, first, count):
@@ -151,6 +153,13 @@
     def rows_of(k):
         return pl.ds(k * CH, CH)
 
+    def sources(first, count=1):
+        return range(first * PER + (first == HOME), (first + count) * PER)
+
+    def others(first, count=1):
+        skip = CAP if first == HOME else 0
+        return pl.ds(first * CH + skip, count * CH - skip)
+
     def block(p):
         return pl.ds(p * CAP, CAP)
 
@@ -172,7 +181,7 @@
         )
 
     def send_gates(k):
-        for p in range(max(k * PER, 1), (k + 1) * PER):
+        for p in sources(k):
             dz, dy = ORDER[p]
             remote(
                 gate_lines.at[p // 8], gate_in.at[p], gl_send.at[0], gl_recv.at[k], exp_of(z - dz, y - dy), h
@@ -187,7 +196,7 @@
             ).start()
 
     def dispatch_near(k):
-        for p in range(max(k * PER, 1), (k + 1) * PER):
+        for p in sources(k):
             dz, dy = ORDER[p]
             remote(
                 near.at[:, block(p + (NEAR.index(k) - k) * PER)], rows.at[c, :, block(p)],
@@ -235,14 +244,14 @@
             wait_recv(raw.at[xo, pl.ds(TOK // 2, TOK // 2)], t_recv.at[3])
         fill_near(k)
         dispatch_near(k)
-        if k == 0:
-            rows[c, :, 0:CAP, :] = near[:, 0:CAP, :]
+        if k == HOME:
+            rows[c, :, HOME * CH:HOME * CH + CAP, :] = near[:, 0:CAP, :]
 
     def part(xx, k, start=0, size=CH):
         return rows.at[c, xx, pl.ds(k * CH + start, size)]
 
-    def whole(cc, k, start=0):
-        return rows.at[cc, :, pl.ds(k * CH + start, CH - start)]
+    def whole(cc, k):
+        return rows.at[cc, :, rows_of(k)]
 
     half = CH // 2
 
@@ -270,8 +279,7 @@
             wait_recv(part(xo, k, half, half), b2_recv.at[k])
             remote(part(xo, k), part(xo, k), gs_send.at[3], gs_recv.at[k, 3], e, sib).start()
         else:
-            start = CAP if k == 0 else 0
-            wait_recv(whole(c, k, start), n_recv.at[k])
+            wait_recv(rows.at[c, :, others(k)], n_recv.at[k])
             remote(whole(c, k), whole(c, k), gs_send.at[4], gs_recv.at[k, 0], e, sib).start()
 
     def gather4(k):
@@ -281,97 +289,102 @@
         else:
             wait_recv(whole(1 - c, k), gs_recv.at[k, 0])
 
-    def eye(k):
-        return lane[0:CH] == sub[0:CH] + k % 2 * CH
+    def eye(first, count):
+        return lane[0:count * CH] == sub[0:count * CH] + first % 2 * CH
 
     def features(hh):
         return pl.ds(pl.multiple_of(hh * FL, FL), FL)
 
-    def compute(k):
-        gather4(k)
-        here = rows_of(k)
-
-        pre = jnp.zeros((CH, HID), F32)
-        back = jnp.zeros((CH, HID), F32)
+    def group_rows(g):
+        first, count = GROUPS[g]
+        return pl.ds(first * CH, count * CH)
+
+    def compute(g):
+        first, count = GROUPS[g]
+        for k in range(first, first + count):
+            gather4(k)
+        here, high = group_rows(g), count * CH
+        pre = jnp.zeros((high, HID), F32)
+        back = jnp.zeros((high, HID), F32)
         for hh in range(HEAD):
             part_of = pl.ds(hh * FL, FL)
             pre = pre + nn(rows[hh % 2, hh // 2, here, 0:FL], wup[part_of, :])
             back = back + nn(rows[hh % 2, hh // 2, here, FL:XD], wdn_t[part_of, :])
-        first = 1 if k == 0 else 0
-        wait_recv(gate_in.at[pl.ds(k * PER + first, PER - first)], gl_recv.at[k])
-        g = jnp.sum(jnp.where(eye(k), merge(gate_in, k * PER, PER), 0.0), axis=1, keepdims=True)
+        for k in range(first, first + count):
+            places = sources(k)
+            wait_recv(gate_in.at[pl.ds(places[0], len(places))], gl_recv.at[k])
+        diagonal = eye(first, count)
+        gate = merge(gate_in, first * PER, count * PER)
+        g_column = jnp.sum(jnp.where(diagonal, gate, 0.0), axis=1, keepdims=True)
         act, slope = gelu_parts(pre)
         score = jnp.sum(back * act, axis=1, keepdims=True)
-        scaled[here, :] = (g * act).astype(BF16)
-        delta[here, :] = (g * back * slope).astype(BF16)
-
+        scaled[here, :] = (g_column * act).astype(BF16)
+        delta[here, :] = (g_column * back * slope).astype(BF16)
         terms = delta[here, :]
         for xx in range(NX):
-            sib_send[k, xx] = nn(terms, wup_t[:, features(xx * 2 + (1 - c))]).astype(BF16)
-        remote(sib_send.at[k], sib_recv.at[k], sib_ss.at[k], sib_rs.at[k], e, sib).start()
-        line = jnp.sum(jnp.where(eye(k), score, 0.0), axis=0, keepdims=True)
-        sc_send[k] = line
-        sc_recv[k, h] = line
+            sib_send[xx, here, :] = nn(terms, wup_t[:, features(xx * 2 + (1 - c))]).astype(BF16)
+        remote(sib_send.at[:, here], sib_recv.at[:, here], sib_ss.at[g], sib_rs.at[g], e, sib).start()
+        line = jnp.sum(jnp.where(diagonal, score, 0.0), axis=0, keepdims=True)
+        sc_send[g] = line
+        sc_recv[g, h] = line
 
         def tell(i, carry):
             remote(
-                sc_send.at[k], sc_recv.at[k, h], sc_ss.at[k], sc_rs.at[k], e, lax.rem(h + i, HEAD)
+                sc_send.at[g], sc_recv.at[g, h], sc_ss.at[g], sc_rs.at[g], e, lax.rem(h + i, HEAD)
             ).start()
             return carry
 
         lax.fori_loop(1, HEAD, tell, 0)
-
         for xx in range(NX):
-            own[k, xx] = nn(terms, wup_t[:, features(xx * 2 + c)])
-
-    def pair(k, xx, start, size):
-        at = lax.rem(xx + NX, NX)
-        cols = pl.ds(start, size)
-        return own[k, at, :, cols] + sib_recv[k, at, :, cols].astype(F32)
+            own[xx, here, :] = nn(terms, wup_t[:, features(xx * 2 + c)])
+
+    def pair(g, xx, start, size):
+        here, cols = group_rows(g), pl.ds(start, size)
+        return own[xx, here, cols] + sib_recv[xx, here, cols].astype(F32)
 
     hf = FL // 2
 
-    def reduce1(k):
-        wait_recv(sib_recv.at[k], sib_rs.at[k])
-        m1s[k, 0] = pair(k, x + 2, 0, hf).astype(BF16)
-        remote(m1s.at[k, 0], m1r.at[k, 0], m1_ss.at[k, 0], m1_rs.at[k, 0], e, right).start()
-        m1s[k, 1] = pair(k, x + 2, hf, hf).astype(BF16)
-        remote(m1s.at[k, 1], m1r.at[k, 1], m1_ss.at[k, 1], m1_rs.at[k, 1], e, left).start()
-
-    def reduce2(k):
-        m2s[k, 0, :, hf:FL] = pair(k, x + 1, hf, hf).astype(BF16)
-        m2s[k, 1, :, 0:hf] = pair(k, x - 1, 0, hf).astype(BF16)
-        wait_recv(m1r.at[k, 0], m1_rs.at[k, 0])
-        m2s[k, 0, :, 0:hf] = (pair(k, x + 1, 0, hf) + m1r[k, 0].astype(F32)).astype(BF16)
-        remote(m2s.at[k, 0], m2r.at[k, 0], m2_ss.at[k, 0], m2_rs.at[k, 0], e, right).start()
-        wait_recv(m1r.at[k, 1], m1_rs.at[k, 1])
-        m2s[k, 1, :, hf:FL] = (pair(k, x - 1, hf, hf) + m1r[k, 1].astype(F32)).astype(BF16)
-        remote(m2s.at[k, 1], m2r.at[k, 1], m2_ss.at[k, 1], m2_rs.at[k, 1], e, left).start()
-
-    def reduce3(k):
-        here = rows_of(k)
-        wait_recv(sc_recv.at[k, pl.ds(0, HEAD - 1)], sc_rs.at[k])
-        total = sc_recv[k, 0]
+    def reduce1(g):
+        here = group_rows(g)
+        wait_recv(sib_recv.at[:, here], sib_rs.at[g])
+        for i, to in enumerate((right, left)):
+            m1s[i, here, :] = pair(g, xo, i * hf, hf).astype(BF16)
+            remote(m1s.at[i, here], m1r.at[i, here], m1_ss.at[g, i], m1_rs.at[g, i], e, to).start()
+
+    def reduce2(g):
+        here = group_rows(g)
+        m2s[0, here, hf:FL] = pair(g, xr, hf, hf).astype(BF16)
+        m2s[1, here, 0:hf] = pair(g, xl, 0, hf).astype(BF16)
+        for i, (at, to) in enumerate(((xr, right), (xl, left))):
+            wait_recv(m1r.at[i, here], m1_rs.at[g, i])
+            both = pair(g, at, i * hf, hf) + m1r[i, here, :].astype(F32)
+            m2s[i, here, i * hf:(i + 1) * hf] = both.astype(BF16)
+            remote(m2s.at[i, here], m2r.at[i, here], m2_ss.at[g, i], m2_rs.at[g, i], e, to).start()
+
+    def reduce3(g):
+        here, (first, count) = group_rows(g), GROUPS[g]
+        wait_recv(sc_recv.at[g, pl.ds(0, HEAD - 1)], sc_rs.at[g])
+        total = sc_recv[g, 0]
         for i in range(1, HEAD):
-            total = total + sc_recv[k, i]
-        score_lines[k] = total.astype(BF16).astype(F32)
-        wait_recv(m2r.at[k, 0], m2_rs.at[k, 0])
-        wait_recv(m2r.at[k, 1], m2_rs.at[k, 1])
-        done = pair(k, x, 0, FL) + m2r[k, 0].astype(F32) + m2r[k, 1].astype(F32)
+            total = total + sc_recv[g, i]
+        score_lines[g] = total.astype(BF16).astype(F32)
+        wait_recv(m2r.at[0, here], m2_rs.at[g, 0])
+        wait_recv(m2r.at[1, here], m2_rs.at[g, 1])
+        done = pair(g, x, 0, FL) + m2r[0, here, :].astype(F32) + m2r[1, here, :].astype(F32)
         ret_send[here, :] = done.astype(BF16)
-
-        for p in range(max(k * PER, 1), (k + 1) * PER):
+        for p in sources(first, count):
             dz, dy = ORDER[p]
             to = exp_of(z + dz, y + dy)
             remote(
-                ret_send.at[block(p)], ret_recv.at[block(p)], r_ss.at[0], r_rs.at[k], to, h
+                ret_send.at[block(p)], ret_recv.at[block(p)], r_ss.at[0], r_rs.at[g], to, h
             ).start()
             remote(
-                score_lines.at[k], score_in.at[p], sl_send.at[0], sl_recv.at[0], to, h
+                score_lines.at[g], score_in.at[p], sl_send.at[0], sl_recv.at[0], to, h
             ).start()
-        if k == 0:
-            ret_recv[0:CAP, :] = ret_send[0:CAP, :]
-            score_in[0] = score_lines[0]
+        if first == HOME:
+            own_rows = pl.ds(HOME * CH, CAP)
+            ret_recv[own_rows, :] = ret_send[own_rows, :]
+            score_in[HOME * PER] = score_lines[g]
 
     def weights_down(k):
         flat = scaled[...].T
@@ -390,12 +403,9 @@
         stages[stage](k)
 
     total = jnp.zeros((TOK, FL), F32)
-    for k in range(NCH):
-        here = rows_of(k)
-        if k == 0:
-            wait_recv(ret_recv.at[pl.ds(CAP, CH - CAP)], r_rs.at[k])
-        else:
-            wait_recv(ret_recv.at[here], r_rs.at[k])
+    for g, (first, count) in enumerate(GROUPS):
+        here = group_rows(g)
+        wait_recv(ret_recv.at[others(first, count)], r_rs.at[g])
         total = total + nn(pt0[:, here] + pt1[:, here], ret_recv[here, :])
     gt_out[...] = total.astype(BF16)
     wait_recv(score_in.at[pl.ds(1, EXP - 1)], sl_recv.at[0])
@@ -424,12 +434,13 @@
     halves = rows.at[0, 0, pl.ds(0, far_rows // 2)]
     wait_send(halves, a2_send.at[0])
     wait_send(halves, b2_send.at[0])
-    for k in range(NCH):
-        wait_send(sib_send.at[k], sib_ss.at[k])
+    for g in range(len(GROUPS)):
+        here = group_rows(g)
+        wait_send(sib_send.at[:, here], sib_ss.at[g])
         for i in range(2):
-            wait_send(m1s.at[k, i], m1_ss.at[k, i])
-            wait_send(m2s.at[k, i], m2_ss.at[k, i])
-        wait_send(sc_recv.at[k, pl.ds(0, HEAD - 1)], sc_ss.at[k])
+            wait_send(m1s.at[i, here], m1_ss.at[g, i])
+            wait_send(m2s.at[i, here], m2_ss.at[g, i])
+        wait_send(sc_recv.at[g, pl.ds(0, HEAD - 1)], sc_ss.at[g])
     wait_send(ret_send.at[pl.ds(CAP, ROWS - CAP)], r_ss.at[0])
 
 
@@ -469,13 +480,13 @@
             pltpu.VMEM((EXP, 1, LINE), F32),
             pltpu.VMEM((ROWS, HID), BF16),
             pltpu.VMEM((ROWS, HID), BF16),
-            pltpu.VMEM((NCH, NX, CH, FL), BF16),
-            pltpu.VMEM((NCH, NX, CH, FL), BF16),
-            pltpu.VMEM((NCH, NX, CH, FL), F32),
-            pltpu.VMEM((NCH, 2, CH, FL // 2), BF16),
-            pltpu.VMEM((NCH, 2, CH, FL // 2), BF16),
-            pltpu.VMEM((NCH, 2, CH, FL), BF16),
-            pltpu.VMEM((NCH, 2, CH, FL), BF16),
+            pltpu.VMEM((NX, ROWS, FL), BF16),
+            pltpu.VMEM((NX, ROWS, FL), BF16),
+            pltpu.VMEM((NX, ROWS, FL), F32),
+            pltpu.VMEM((2, ROWS, FL // 2), BF16),
+            pltpu.VMEM((2, ROWS, FL // 2), BF16),
+            pltpu.VMEM((2, ROWS, FL), BF16),
+            pltpu.VMEM((2, ROWS, FL), BF16),
             pltpu.VMEM((NCH, 1, LINE), F32),
             pltpu.VMEM((NCH, HEAD, 1, LINE), F32),
             pltpu.VMEM((ROWS, FL), BF16),

time: 83 us -> 77.5 us (0.934)
  Pallas kernels: 81.5 us -> 76 us
    pallas_call x1, Pallas kernels: 79.4 us -> 73.9 us  [shards(): pl.pallas_call(kernel, out_shape=tuple((pltpu.VMEM(shape, BF16) for shape...]
where the time goes in v4:
time: 77.5 us; the launch traced here: 76.8 us
  Pallas kernels  76 us (98%)
  between operations  0.8 us (1%)
    pallas_call x1, Pallas kernels, shards(): pl.pallas_call(kernel, out_shape=tuple((pltpu.VMEM(shape, BF16) for shape...  73.9 us
    pallas_call x1, Pallas kernels, shards(): pl.pallas_call(store, out_shape=tuple((jax.ShapeDtypeStruct(shape, BF16)...  2.09 us

profile of v4, /device:TPU:2, one launch (start us, length us, event | category | flops | bytes accessed | tf_op | source)
XLA Modules:
  0.0 76.8 jit_solution(4959927739025581494)
XLA Ops:
  0.6 73.9 %shard_map.93 = (bf16[128,512]{1,0:T(8,128)(2,1)S(1)}, bf16[2,128]{1,0:T(2,128)(2,1)S(1)}, bf16[1,4096,256]{2,1,0:T(8,128)(2,1)S(1)}, bf16[1,256,4096]{2,1,0:T(8,128)(2,1)S(1)}) custom-call(bf16[128,512]{1,0:T(8,128)(2,1)} %tok_ref.1, bf16[128,512]{1,0:T(8,128)(2,1)} %cot_ref.1, bf16[2,128]{1,0:T(2,128)(2,1)} %bitcast.4, s32[2,128]{1,0:T(2,128)} %bitcast.3, ...), custom_call_target="tpu_custom_call" | custom-call | flops 5368709120 | bytes 8388608 | tf_op jit(solution)/shard_map/pallas_call | solution.py:461
  74.6 2.1 %shard_map.94 = (bf16[128,512]{1,0:T(8,128)(2,1)}, bf16[2,128]{1,0:T(2,128)(2,1)}, bf16[1,4096,256]{2,1,0:T(8,128)(2,1)}, bf16[1,256,4096]{2,1,0:T(8,128)(2,1)}) custom-call(bf16[128,512]{1,0:T(8,128)(2,1)S(1)} %get-tuple-element.12.refs_0_, bf16[2,128]{1,0:T(2,128)(2,1)S(1)} %get-tuple-element.13.refs_1_, ...), custom_call_target="tpu_custom_call" | custom-call | tf_op jit(solution)/shard_map/pallas_call | solution.py:518

commit v5 on v4

--- a/solution.py
+++ b/solution.py
@@ -41,17 +41,17 @@
 HOME = 2
 NEAR = (HOME, 5, 7)
 FAR = (0, 1, 3, 4, 6)
-AHEAD = 3
+AHEAD = 2
 GROUPS = ((0, 1), (1, 1), (2, 1), (3, 1), (4, 1), (5, 1), (6, 1), (7, 1))
 PLAN = (
-    ("g1", 0), ("d", 4), ("pass", 0), ("g2", 0), ("g1", 1), ("d", 6), ("near", 2), ("g3", 0),
-    ("g1", 3), ("near", 5), ("g2", 1), ("c", 0), ("g2", 3), ("g3", 1), ("g1", 4), ("near", 7),
-    ("r1", 0), ("g3", 2), ("g3", 3), ("c", 1), ("g1", 6), ("c", 2), ("g2", 4), ("r2", 0),
-    ("r1", 1), ("c", 3), ("g2", 6), ("r1", 2), ("g3", 5), ("g3", 4), ("r1", 3), ("r3", 0),
-    ("r2", 1), ("g3", 6), ("c", 4), ("r2", 2), ("r2", 3), ("g3", 7), ("c", 5), ("r1", 4),
-    ("c", 6), ("c", 7), ("r2", 4), ("r1", 5), ("r3", 1), ("r1", 6), ("r3", 2), ("r3", 3),
-    ("r1", 7), ("r2", 5), ("r2", 6), ("r3", 4), ("r2", 7), ("wd", 0), ("r3", 5), ("r3", 6),
-    ("r3", 7), ("wu", 0),
+    ("g1", 0), ("d", 3), ("pass", 0), ("g2", 0), ("g1", 1), ("d", 4), ("near", 2), ("g3", 0),
+    ("g1", 3), ("d", 6), ("near", 5), ("g2", 1), ("c", 0), ("g2", 3), ("g3", 1), ("g1", 4),
+    ("near", 7), ("r1", 0), ("g3", 2), ("g3", 3), ("c", 1), ("g1", 6), ("c", 2), ("g2", 4),
+    ("r2", 0), ("r1", 1), ("c", 3), ("g2", 6), ("r1", 2), ("g3", 5), ("g3", 4), ("r1", 3),
+    ("r3", 0), ("r2", 1), ("g3", 6), ("c", 4), ("r2", 2), ("r2", 3), ("g3", 7), ("c", 5),
+    ("r1", 4), ("c", 6), ("c", 7), ("r2", 4), ("r1", 5), ("r3", 1), ("r1", 6), ("r3", 2),
+    ("r3", 3), ("r1", 7), ("r2", 5), ("r2", 6), ("r3", 4), ("r2", 7), ("wd", 0), ("r3", 5),
+    ("r3", 6), ("r3", 7), ("wu", 0),
 )
 
 

time: 77.5 us -> 76.6 us (0.988)
  no operation moved by 1% of the time
where the time goes in v5:
time: 76.6 us; the launch traced here: 76.1 us
  Pallas kernels  75.3 us (98%)
  between operations  0.8 us (1%)
    pallas_call x1, Pallas kernels, shards(): pl.pallas_call(kernel, out_shape=tuple((pltpu.VMEM(shape, BF16) for shape...  73.2 us
    pallas_call x1, Pallas kernels, shards(): pl.pallas_call(store, out_shape=tuple((jax.ShapeDtypeStruct(shape, BF16)...  2.09 us

profile of v5, /device:TPU:2, one launch (start us, length us, event | category | flops | bytes accessed | tf_op | source)
XLA Modules:
  0.0 76.1 jit_solution(1764646232210567474)
XLA Ops:
  0.6 73.2 %shard_map.93 = (bf16[128,512]{1,0:T(8,128)(2,1)S(1)}, bf16[2,128]{1,0:T(2,128)(2,1)S(1)}, bf16[1,4096,256]{2,1,0:T(8,128)(2,1)S(1)}, bf16[1,256,4096]{2,1,0:T(8,128)(2,1)S(1)}) custom-call(bf16[128,512]{1,0:T(8,128)(2,1)} %tok_ref.1, bf16[128,512]{1,0:T(8,128)(2,1)} %cot_ref.1, bf16[2,128]{1,0:T(2,128)(2,1)} %bitcast.4, s32[2,128]{1,0:T(2,128)} %bitcast.3, ...), custom_call_target="tpu_custom_call" | custom-call | flops 5368709120 | bytes 8388608 | tf_op jit(solution)/shard_map/pallas_call | solution.py:461
  73.8 2.1 %shard_map.94 = (bf16[128,512]{1,0:T(8,128)(2,1)}, bf16[2,128]{1,0:T(2,128)(2,1)}, bf16[1,4096,256]{2,1,0:T(8,128)(2,1)}, bf16[1,256,4096]{2,1,0:T(8,128)(2,1)}) custom-call(bf16[128,512]{1,0:T(8,128)(2,1)S(1)} %get-tuple-element.12.refs_0_, bf16[2,128]{1,0:T(2,128)(2,1)S(1)} %get-tuple-element.13.refs_1_, ...), custom_call_target="tpu_custom_call" | custom-call | tf_op jit(solution)/shard_map/pallas_call | solution.py:518

commit v6 on v5

--- a/solution.py
+++ b/solution.py
@@ -444,9 +444,19 @@
     wait_send(ret_send.at[pl.ds(CAP, ROWS - CAP)], r_ss.at[0])
 
 
+CUTS = 4
+
+
 def store(*refs):
     ins, outs, sem = refs[:4], refs[4:8], refs[8]
-    copies = [pltpu.make_async_copy(ins[i], outs[i], sem.at[i]) for i in range(4)]
+    pairs = []
+    for i in (2, 3):
+        height = ins[i].shape[1] // CUTS
+        for j in range(CUTS):
+            here = pl.ds(j * height, height)
+            pairs.append((ins[i].at[:, here], outs[i].at[:, here]))
+    pairs += [(ins[i], outs[i]) for i in (0, 1)]
+    copies = [pltpu.make_async_copy(src, dst, sem.at[i]) for i, (src, dst) in enumerate(pairs)]
     for one in copies:
         one.start()
     for one in copies:
@@ -520,7 +530,7 @@
         out_shape=tuple(jax.ShapeDtypeStruct(shape, BF16) for shape in shapes),
         in_specs=[vmem] * 4,
         out_specs=(hbm,) * 4,
-        scratch_shapes=[dma((4,))],
+        scratch_shapes=[dma((2 * CUTS + 2,))],
         compiler_params=pltpu.CompilerParams(vmem_limit_bytes=16 * 1024 * 1024),
     )(*results)
     return grad_tokens, grad_gates.T, grad_up, grad_down

time: 76.6 us -> 76.6 us (level)
  no operation moved by 1% of the time
where the time goes in v6:
time: 76.6 us; the launch traced here: 76.1 us
  Pallas kernels  75.3 us (98%)
  between operations  0.8 us (1%)
    pallas_call x1, Pallas kernels, shards(): pl.pallas_call(kernel, out_shape=tuple((pltpu.VMEM(shape, BF16) for shape...  73.2 us
    pallas_call x1, Pallas kernels, shards(): pl.pallas_call(store, out_shape=tuple((jax.ShapeDtypeStruct(shape, BF16)...  2.13 us

profile of v6, /device:TPU:2, one launch (start us, length us, event | category | flops | bytes accessed | tf_op | source)
XLA Modules:
  0.0 76.1 jit_solution(15382797573630855610)
XLA Ops:
  0.6 73.2 %shard_map.93 = (bf16[128,512]{1,0:T(8,128)(2,1)S(1)}, bf16[2,128]{1,0:T(2,128)(2,1)S(1)}, bf16[1,4096,256]{2,1,0:T(8,128)(2,1)S(1)}, bf16[1,256,4096]{2,1,0:T(8,128)(2,1)S(1)}) custom-call(bf16[128,512]{1,0:T(8,128)(2,1)} %tok_ref.1, bf16[128,512]{1,0:T(8,128)(2,1)} %cot_ref.1, bf16[2,128]{1,0:T(2,128)(2,1)} %bitcast.4, s32[2,128]{1,0:T(2,128)} %bitcast.3, ...), custom_call_target="tpu_custom_call" | custom-call | flops 5368709120 | bytes 8388608 | tf_op jit(solution)/shard_map/pallas_call | solution.py:471
  73.8 2.1 %shard_map.94 = (bf16[128,512]{1,0:T(8,128)(2,1)}, bf16[2,128]{1,0:T(2,128)(2,1)}, bf16[1,4096,256]{2,1,0:T(8,128)(2,1)}, bf16[1,256,4096]{2,1,0:T(8,128)(2,1)}) custom-call(bf16[128,512]{1,0:T(8,128)(2,1)S(1)} %get-tuple-element.12.refs_0_, bf16[2,128]{1,0:T(2,128)(2,1)S(1)} %get-tuple-element.13.refs_1_, ...), custom_call_target="tpu_custom_call" | custom-call | tf_op jit(solution)/shard_map/pallas_call | solution.py:528
